TPU v7x, 32 devices: a whole 2x2x4 slice. The times are simulated.
32 devices in a mesh: dp: 8 (over y, x, core), fsdp: 4 (over z).
Axes of the slice: x: 2, y: 2, z: 4, core: 2. Of those that a mesh axis runs over, the one named last changes fastest.
Arguments:
- tokens: bfloat16 [32768, 768], P(('dp', 'fsdp')), may hold values from -6 to 6
- segment_ids: int32 [32, 1024], P(('dp', 'fsdp')), may hold values from 0 to 5, never falling along the last dimension, each value on 1 to 512 neighbouring positions
- cotangent: bfloat16 [32768, 768], P(('dp', 'fsdp')), may hold values from -6 to 6
- projector: bfloat16 [768, 2304], P(('dp', 'fsdp')), may hold values from -0.21875 to 0.21875
- combiner: bfloat16 [768, 768], P(('dp', 'fsdp')), may hold values from -0.875 to 0.875
- attend_bias: bfloat16 [768], P(('dp', 'fsdp')), may hold values from -1.796875 to 1.796875
- expander: bfloat16 [768, 3072], P(('dp', 'fsdp')), may hold values from -0.21875 to 0.21875
- expand_bias: bfloat16 [3072], P(('dp', 'fsdp')), may hold values from -1.796875 to 1.796875
- reducer: bfloat16 [3072, 768], P(('dp', 'fsdp')), may hold values from -0.109375 to 0.109375
- reduce_bias: bfloat16 [768], P(('dp', 'fsdp')), may hold values from -1.796875 to 1.796875
- first_gain: bfloat16 [768], P(('dp', 'fsdp')), may hold values from 0.5 to 1.5
- first_shift: bfloat16 [768], P(('dp', 'fsdp')), may hold values from -1.796875 to 1.796875
- second_gain: bfloat16 [768], P(('dp', 'fsdp')), may hold values from 0.5 to 1.5
- second_shift: bfloat16 [768], P(('dp', 'fsdp')), may hold values from -1.796875 to 1.796875
Outputs:
- layer_output: bfloat16 [32768, 768], P(('dp', 'fsdp'))
- grad_tokens: float32 [32768, 768], P(('dp', 'fsdp'))
- grad_projector: float32 [768, 2304], P(('dp', 'fsdp'))
- grad_combiner: float32 [768, 768], P(('dp', 'fsdp'))
- grad_attend_bias: float32 [768], P(('dp', 'fsdp'))
- grad_expander: float32 [768, 3072], P(('dp', 'fsdp'))
- grad_expand_bias: float32 [3072], P(('dp', 'fsdp'))
- grad_reducer: float32 [3072, 768], P(('dp', 'fsdp'))
- grad_reduce_bias: float32 [768], P(('dp', 'fsdp'))
- grad_first_gain: float32 [768], P(('dp', 'fsdp'))
- grad_first_shift: float32 [768], P(('dp', 'fsdp'))
- grad_second_gain: float32 [768], P(('dp', 'fsdp'))
- grad_second_shift: float32 [768], P(('dp', 'fsdp'))
Inputs may be any that keep to these rules, and one draw needn't show every extreme that they name: `segment_ids`: within each window the ids never fall; an id covers 1 to 512 consecutive positions, and some id exactly that many.
All inputs are finite; a program needn't handle non-finite values.
Results may differ from a plain program's by a relative error of at most 0.0092.
Values may be sent and summed in bfloat16 or wider, within the bound.
No kernel may reach another device: no remote copies, remote signals or barrier semaphores. Data moves between devices by JAX's collectives and lax.ppermute only.
A program may use at most 192 MiB of HBM per device.

v0:
```python
import math

import jax
import jax.numpy as jnp
from jax import lax
from jax.sharding import PartitionSpec as P

D = 768
HEADS = 24
HD = 32
WIN = 1024


epsilon = 1e-05
masked_score = -1000000000.0


def layer_norm(values, gain_vec, shift_vec):
    average = jnp.mean(values, axis=-1, keepdims=True)
    centred = values - average
    variance = jnp.mean(centred * centred, axis=-1, keepdims=True)
    return centred * lax.rsqrt(variance + epsilon) * gain_vec + shift_vec


def masked_scores(queries, key_rows, episode):
    scores = jnp.einsum(
        "qe,ke->qk", queries, key_rows, preferred_element_type=jnp.float32
    ) * HD ** (-0.5)
    positions = jnp.arange(queries.shape[0])
    allowed = (episode[:, None] == episode[None, :]) & (positions[:, None] >= positions[None, :])
    return jnp.where(allowed, scores, masked_score)


def attend_forward(member):
    queries, key_rows, value_rows, episode = member
    scores = masked_scores(queries, key_rows, episode)
    maximum = jnp.max(scores, axis=-1, keepdims=True)
    exponent = jnp.exp(scores - maximum)
    totals = jnp.sum(exponent, axis=-1, keepdims=True)
    probability = (exponent / totals).astype(jnp.bfloat16)
    attended = jnp.einsum("qk,ke->qe", probability, value_rows, preferred_element_type=jnp.float32)
    return (attended.astype(jnp.bfloat16), (maximum + jnp.log(totals))[:, 0])


def attend_backward(member):
    queries, key_rows, value_rows, episode, log_total, grad_out = member
    scores = masked_scores(queries, key_rows, episode)
    probability = jnp.exp(scores - log_total[:, None])
    grad_prob = jnp.einsum("qe,ke->qk", grad_out, value_rows, preferred_element_type=jnp.float32)
    row_dot = jnp.sum(grad_prob * probability, axis=-1, keepdims=True)
    grad_score = (probability * (grad_prob - row_dot)).astype(jnp.bfloat16)
    grad_values = jnp.einsum(
        "qk,qe->ke", probability.astype(jnp.bfloat16), grad_out, preferred_element_type=jnp.float32
    )
    grad_queries = jnp.einsum(
        "qk,ke->qe", grad_score, key_rows, preferred_element_type=jnp.float32
    ) * HD ** (-0.5)
    grad_keys = jnp.einsum(
        "qk,qe->ke", grad_score, queries, preferred_element_type=jnp.float32
    ) * HD ** (-0.5)
    return jnp.stack(
        [
            grad_queries.astype(jnp.bfloat16),
            grad_keys.astype(jnp.bfloat16),
            grad_values.astype(jnp.bfloat16),
        ]
    )


def body(
    tokens,
    segment_ids,
    cotangent,
    projector,
    combiner,
    attend_bias,
    expander,
    expand_bias,
    reducer,
    reduce_bias,
    first_gain,
    first_shift,
    second_gain,
    second_shift,
):
    gathered = (
        lax.all_gather(projector, ("dp", "fsdp"), axis=0, tiled=True),
        lax.all_gather(combiner, ("dp", "fsdp"), axis=0, tiled=True),
        lax.all_gather(attend_bias, ("dp", "fsdp"), axis=0, tiled=True),
        lax.all_gather(expander, ("dp", "fsdp"), axis=0, tiled=True),
        lax.all_gather(expand_bias, ("dp", "fsdp"), axis=0, tiled=True),
        lax.all_gather(reducer, ("dp", "fsdp"), axis=0, tiled=True),
        lax.all_gather(reduce_bias, ("dp", "fsdp"), axis=0, tiled=True),
        lax.all_gather(first_gain, ("dp", "fsdp"), axis=0, tiled=True),
        lax.all_gather(first_shift, ("dp", "fsdp"), axis=0, tiled=True),
        lax.all_gather(second_gain, ("dp", "fsdp"), axis=0, tiled=True),
        lax.all_gather(second_shift, ("dp", "fsdp"), axis=0, tiled=True),
    )
    (
        full_proj,
        full_comb,
        bias_attend,
        full_expand,
        bias_expand,
        full_reduce,
        bias_reduce,
        gain_one,
        shift_one,
        gain_two,
        shift_two,
    ) = gathered
    tok_count = tokens.shape[0]
    windows = tok_count // WIN
    count = windows * HEADS
    inputs = tokens.astype(jnp.float32)
    normed_one = layer_norm(
        inputs, gain_one.astype(jnp.float32), shift_one.astype(jnp.float32)
    ).astype(jnp.bfloat16)
    project = jnp.dot(normed_one, full_proj, preferred_element_type=jnp.float32).astype(
        jnp.bfloat16
    )
    split = (
        project.reshape(windows, WIN, 3, HEADS, HD)
        .transpose(2, 0, 3, 1, 4)
        .reshape(3, count, WIN, HD)
    )
    episode = jnp.repeat(segment_ids, HEADS, axis=0)
    head_out, log_total = lax.map(attend_forward, (split[0], split[1], split[2], episode))
    attended = head_out.reshape(windows, HEADS, WIN, HD).transpose(0, 2, 1, 3).reshape(tok_count, D)
    branch = jnp.dot(attended, full_comb, preferred_element_type=jnp.float32) + bias_attend.astype(
        jnp.float32
    )
    middle = inputs + branch
    row_block = math.gcd(512, tok_count)
    blocks = tok_count // row_block
    middle_blocks = middle.reshape(blocks, row_block, D)

    def ffn_forward(middle_block):
        normed = layer_norm(
            middle_block, gain_two.astype(jnp.float32), shift_two.astype(jnp.float32)
        ).astype(jnp.bfloat16)
        upper = jnp.dot(
            normed, full_expand, preferred_element_type=jnp.float32
        ) + bias_expand.astype(jnp.float32)
        active = jax.nn.gelu(upper).astype(jnp.bfloat16)
        lowered = jnp.dot(
            active, full_reduce, preferred_element_type=jnp.float32
        ) + bias_reduce.astype(jnp.float32)
        return (middle_block + lowered).astype(jnp.bfloat16)

    layer_output = lax.map(ffn_forward, middle_blocks).reshape(tok_count, D)
    again = (
        lax.all_gather(projector, ("dp", "fsdp"), axis=0, tiled=True),
        lax.all_gather(combiner, ("dp", "fsdp"), axis=0, tiled=True),
        lax.all_gather(attend_bias, ("dp", "fsdp"), axis=0, tiled=True),
        lax.all_gather(expander, ("dp", "fsdp"), axis=0, tiled=True),
        lax.all_gather(expand_bias, ("dp", "fsdp"), axis=0, tiled=True),
        lax.all_gather(reducer, ("dp", "fsdp"), axis=0, tiled=True),
        lax.all_gather(reduce_bias, ("dp", "fsdp"), axis=0, tiled=True),
        lax.all_gather(first_gain, ("dp", "fsdp"), axis=0, tiled=True),
        lax.all_gather(first_shift, ("dp", "fsdp"), axis=0, tiled=True),
        lax.all_gather(second_gain, ("dp", "fsdp"), axis=0, tiled=True),
        lax.all_gather(second_shift, ("dp", "fsdp"), axis=0, tiled=True),
    )
    (
        back_proj,
        back_comb,
        unused_bias,
        back_expand,
        back_bias_expand,
        back_reduce,
        unused_reduce,
        back_gain_one,
        back_shift_one,
        back_gain_two,
        back_shift_two,
    ) = again
    gain_first = back_gain_one.astype(jnp.float32)
    shift_first = back_shift_one.astype(jnp.float32)
    gain_second = back_gain_two.astype(jnp.float32)
    shift_second = back_shift_two.astype(jnp.float32)
    expand_offset = back_bias_expand.astype(jnp.float32)
    cotangent_blocks = cotangent.reshape(blocks, row_block, D)

    def ffn_back(running, inputs_pair):
        acc_up, acc_bup, acc_down, acc_bdown, acc_gain, acc_shift = running
        middle_block, grad_out = inputs_pair
        normed, norm_pull = jax.vjp(layer_norm, middle_block, gain_second, shift_second)
        normed_low = normed.astype(jnp.bfloat16)
        upper = jnp.dot(normed_low, back_expand, preferred_element_type=jnp.float32) + expand_offset
        active, gelu_pull = jax.vjp(jax.nn.gelu, upper)
        active_low = active.astype(jnp.bfloat16)
        acc_down = acc_down + jnp.einsum(
            "tf,td->fd", active_low, grad_out, preferred_element_type=jnp.float32
        )
        acc_bdown = acc_bdown + jnp.sum(grad_out.astype(jnp.float32), axis=0)
        grad_active = jnp.einsum(
            "td,fd->tf", grad_out, back_reduce, preferred_element_type=jnp.float32
        )
        grad_upper = gelu_pull(grad_active)[0].astype(jnp.bfloat16)
        acc_up = acc_up + jnp.einsum(
            "td,tf->df", normed_low, grad_upper, preferred_element_type=jnp.float32
        )
        acc_bup = acc_bup + jnp.sum(grad_upper.astype(jnp.float32), axis=0)
        grad_normed = jnp.einsum(
            "tf,df->td", grad_upper, back_expand, preferred_element_type=jnp.float32
        )
        grad_mid, grad_gain, grad_shift = norm_pull(grad_normed)
        updated = (
            acc_up,
            acc_bup,
            acc_down,
            acc_bdown,
            acc_gain + grad_gain,
            acc_shift + grad_shift,
        )
        return (updated, grad_out.astype(jnp.float32) + grad_mid)

    width = back_expand.shape[1]
    start_acc = (
        jnp.zeros((D, width), jnp.float32),
        jnp.zeros((width,), jnp.float32),
        jnp.zeros((width, D), jnp.float32),
        jnp.zeros((D,), jnp.float32),
        jnp.zeros((D,), jnp.float32),
        jnp.zeros((D,), jnp.float32),
    )
    ffn_grads, grad_blocks = lax.scan(ffn_back, start_acc, (middle_blocks, cotangent_blocks))
    grad_expand, grad_bexpand, grad_reduce, grad_breduce, grad_gain_two, grad_shift_two = ffn_grads
    grad_middle = grad_blocks.reshape(tok_count, D)
    grad_branch = grad_middle.astype(jnp.bfloat16)
    grad_battend = jnp.sum(grad_branch.astype(jnp.float32), axis=0)
    grad_comb = jnp.einsum("te,td->ed", attended, grad_branch, preferred_element_type=jnp.float32)
    grad_attended = jnp.einsum(
        "td,ed->te", grad_branch, back_comb, preferred_element_type=jnp.float32
    ).astype(jnp.bfloat16)
    grad_heads = (
        grad_attended.reshape(windows, WIN, HEADS, HD).transpose(0, 2, 1, 3).reshape(count, WIN, HD)
    )
    grad_split = lax.map(
        attend_backward, (split[0], split[1], split[2], episode, log_total, grad_heads)
    )
    grad_project = (
        grad_split.reshape(windows, HEADS, 3, WIN, HD)
        .transpose(0, 3, 2, 1, 4)
        .reshape(tok_count, 3 * D)
    )
    grad_proj = jnp.einsum(
        "td,te->de", normed_one, grad_project, preferred_element_type=jnp.float32
    )
    grad_normed_one = jnp.einsum(
        "te,de->td", grad_project, back_proj, preferred_element_type=jnp.float32
    )
    normed_again, first_pull = jax.vjp(layer_norm, inputs, gain_first, shift_first)
    grad_inputs, grad_gain_one, grad_shift_one = first_pull(grad_normed_one)
    grad_tokens = grad_middle + grad_inputs
    owned = (
        lax.psum_scatter(grad_proj, ("dp", "fsdp"), scatter_dimension=0, tiled=True),
        lax.psum_scatter(grad_comb, ("dp", "fsdp"), scatter_dimension=0, tiled=True),
        lax.psum_scatter(grad_battend, ("dp", "fsdp"), scatter_dimension=0, tiled=True),
        lax.psum_scatter(grad_expand, ("dp", "fsdp"), scatter_dimension=0, tiled=True),
        lax.psum_scatter(grad_bexpand, ("dp", "fsdp"), scatter_dimension=0, tiled=True),
        lax.psum_scatter(grad_reduce, ("dp", "fsdp"), scatter_dimension=0, tiled=True),
        lax.psum_scatter(grad_breduce, ("dp", "fsdp"), scatter_dimension=0, tiled=True),
        lax.psum_scatter(grad_gain_one, ("dp", "fsdp"), scatter_dimension=0, tiled=True),
        lax.psum_scatter(grad_shift_one, ("dp", "fsdp"), scatter_dimension=0, tiled=True),
        lax.psum_scatter(grad_gain_two, ("dp", "fsdp"), scatter_dimension=0, tiled=True),
        lax.psum_scatter(grad_shift_two, ("dp", "fsdp"), scatter_dimension=0, tiled=True),
    )
    return (
        layer_output,
        grad_tokens,
        owned[0],
        owned[1],
        owned[2],
        owned[3],
        owned[4],
        owned[5],
        owned[6],
        owned[7],
        owned[8],
        owned[9],
        owned[10],
    )


def solution(mesh):
    return jax.shard_map(
        body,
        mesh=mesh,
        in_specs=(
            P(("dp", "fsdp"), None),
            P(("dp", "fsdp"), None),
            P(("dp", "fsdp"), None),
            P(("dp", "fsdp"), None),
            P(("dp", "fsdp"), None),
            P(("dp", "fsdp")),
            P(("dp", "fsdp"), None),
            P(("dp", "fsdp")),
            P(("dp", "fsdp"), None),
            P(("dp", "fsdp")),
            P(("dp", "fsdp")),
            P(("dp", "fsdp")),
            P(("dp", "fsdp")),
            P(("dp", "fsdp")),
        ),
        out_specs=(
            P(("dp", "fsdp"), None),
            P(("dp", "fsdp"), None),
            P(("dp", "fsdp"), None),
            P(("dp", "fsdp"), None),
            P(("dp", "fsdp")),
            P(("dp", "fsdp"), None),
            P(("dp", "fsdp")),
            P(("dp", "fsdp"), None),
            P(("dp", "fsdp")),
            P(("dp", "fsdp")),
            P(("dp", "fsdp")),
            P(("dp", "fsdp")),
            P(("dp", "fsdp")),
        ),
        check_vma=False,
    )
```

profile of v0, /device:TPU:0, one launch (start us, length us, event | category | flops | bytes accessed | tf_op | source)
XLA Modules:
  0.0 1136.3 jit_solution(3013531136294332353)
XLA Ops:
  16.0 43.0 %all-reduce.15 = (bf16[768]{0:T(1024)(128)(2,1)S(1)}, bf16[768]{0:T(1024)(128)(2,1)S(1)}, bf16[768]{0:T(1024)(128)(2,1)S(1)}, bf16[768]{0:T(1024)(128)(2,1)S(1)}...) all-reduce(bf16[768]{0:T(1024)(128)(2,1)S(1)} %dynamic-update-slice, ...), channel_id=1, replica_groups=mesh['dp'=8,'fsdp'=4] {'dp','fsdp'}, use_global_device_ids=true, to_apply=%add.1 | all-reduce | flops 7680 | bytes 30720
  61.5 12.2 %all-gather.5.cloned.1.call-done = bf16[768,2304]{1,0:T(8,128)(2,1)} async-done(((bf16[24,2304]{1,0:T(8,128)(2,1)}), bf16[768,2304]{1,0:T(8,128)(2,1)}) %all-gather.5.cloned.1.call-update) | async-done | bytes 3538960 | tf_op jit(solution)/shard_map/all_gather | solution.py:87
  73.7 7.9 convolution_convert_fusion
  81.7 6.7 copy.38
  88.3 4.2 slice_bitcast_fusion
  92.5 6.2 copy.39
  98.8 4.5 copy.40
  103.3 4.5 copy.41
  107.8 219.3 %while.57 = (s32[]{:T(128)}, bf16[24,1024,32]{1,2,0:T(8,128)(2,1)S(1)}, f32[24,1024]{1,0:T(8,128)}, s32[24,1024]{1,0:T(8,128)S(1)}, bf16[24,1024,32]{2,1,0:T(8,1...) while((s32[]{:T(128)}, ...), condition=%wide.region_5.6_spmd, body=%wide.region_2.5_spmd.sunk | while | flops 145783808 | bytes 30271616 | solution.py:128
  113.9 3.2 fusion.173
  123.1 3.1 fusion.173
  132.3 3.0 fusion.173
  141.4 3.0 fusion.173
  150.5 3.0 fusion.173
  159.6 3.1 fusion.173
  168.8 3.0 fusion.173
  178.0 3.1 fusion.173
  187.1 3.1 fusion.173
  196.3 3.0 fusion.173
  205.4 3.0 fusion.173
  214.5 3.0 fusion.173
  223.6 3.0 fusion.173
  232.8 3.0 fusion.173
  241.9 3.0 fusion.173
  251.0 3.1 fusion.173
  260.2 3.0 fusion.173
  269.3 3.0 fusion.173
  278.4 3.0 fusion.173
  287.6 3.0 fusion.173
  296.7 3.0 fusion.173
  305.8 3.0 fusion.173
  314.9 3.0 fusion.173
  324.0 3.0 fusion.173
  328.3 3.7 convert_add_fusion.1
  332.0 76.9 %while.60 = (s32[]{:T(128)}, f32[768,3072]{1,0:T(8,128)}, f32[3072]{0:T(1024)S(1)}, f32[3072,768]{1,0:T(8,128)}, f32[768]{0:T(1024)S(1)}, /*index=5*/f32[768]{0:...) while((s32[]{:T(128)}, f32[768,3072]{1,0:T(8,128)}, ...), condition=%wide.region_19.20_spmd.clone, body=%wide.region_10.19_spmd.clone.sunk | while | flops 12154315776 | bytes 179489680 | solution.py:228
  334.1 4.8 fusion.196
  339.0 6.6 convert_reduce_fusion.7
  345.6 3.0 multiply_reduce_fusion.10
  350.6 7.4 select_add_fusion.12
  358.0 10.2 select_add_fusion.14
  370.2 4.8 fusion.196
  375.1 6.6 convert_reduce_fusion.7
  381.7 3.0 multiply_reduce_fusion.10
  386.8 8.8 select_add_fusion.12
  395.6 13.0 %select_add_fusion.14 = f32[3072,768]{1,0:T(8,128)} fusion(f32[3072,768]{1,0:T(8,128)} %get-tuple-element.880, pred[]{:T(512)S(6)} %compare.3, f32[512,3072]{1,0:T(8,128)} %copy-done.29, f32[3072]{0:T(1024)S(1)} %get-tuple-element.908, bf16[2,512,768]{2,1,0:T(8,128)(2,1)S(1)} %copy-done.3, s32[]{:T(128)} %get-tuple-element.877), kind=kOutput, calls=%fused_computation.87.clone.1 | convolution fusion | flops 2436366336 | bytes 25964548 | tf_op jit(solution)/shard_map/while/body/eval_jaxpr/tf,td->fd/dot_general | solution.py:193
  408.9 4.6 convert_reduce_fusion.3
  413.5 2.6 convolution_convert_fusion.1
  416.1 6.3 copy.42
  422.4 4.7 fusion.121
  427.1 289.6 %while.59 = (s32[]{:T(128)}, bf16[24,3,1024,32]{2,3,0,1:T(8,128)(2,1)}, s32[24,1024]{1,0:T(8,128)}, bf16[24,1024,32]{2,1,0:T(8,128)(2,1)}, bf16[24,1024,32]{2,1,...) while((s32[]{:T(128)}, ...), condition=%wide.region_22.23_spmd, body=%wide.region_20.22_spmd.sunk | while | flops 348879872 | bytes 33923172 | solution.py:240
  440.8 2.1 subtract_exponential_fusion.3
  452.9 2.1 subtract_exponential_fusion.3
  464.9 2.1 subtract_exponential_fusion.3
  501.2 2.1 subtract_exponential_fusion.3
  716.8 10.0 fusion.114
  728.4 8.6 fusion.118
  738.8 39.4 %all-reduce.14 = (f32[768]{0:T(1024)S(1)}, f32[3072]{0:T(1024)S(1)}, f32[768]{0:T(1024)S(1)}, f32[768]{0:T(1024)S(1)}, f32[768]{0:T(1024)S(1)}, /*index=5*/f32[768]{0:T(1024)S(1)}, f32[768]{0:T(1024)S(1)}) all-reduce(f32[768]{0:T(1024)S(1)} %get-tuple-element.521, ...), channel_id=4, replica_groups=mesh['dp'=8,'fsdp'=4] {'dp','fsdp'}, use_global_device_ids=true, to_apply=%region_28.29.clone | all-reduce | flops 7680 | bytes 61440
  782.3 5.1 bitcast_add_fusion.1
  787.4 21.6 %while.58 = (s32[]{:T(128)}, bf16[2,512,768]{2,1,0:T(8,128)(2,1)}, f32[2,512,768]{2,1,0:T(8,128)S(1)}, bf16[768]{0:T(1024)(128)(2,1)S(1)}, bf16[768]{0:T(1024)(1...) while((s32[]{:T(128)}, bf16[2,512,768]{2,1,0:T(8,128)(2,1)}, ...), condition=%wide.region_9.10_spmd, body=%wide.region_6.9_spmd.sunk | while | flops 4852291584 | bytes 16588397 | solution.py:151
  787.9 10.2 fusion.176
  798.7 10.3 fusion.176
  809.0 36.5 %reduce-scatter.5.cloned.1.call-done = f32[24,2304]{1,0:T(8,128)} async-done(((f32[768,2304]{1,0:T(8,128)}), f32[24,2304]{1,0:T(8,128)}) %reduce-scatter.5.cloned.1.call-update) | async-done | bytes 221200 | tf_op jit(solution)/shard_map/reduce_scatter | solution.py:258
  845.4 141.5 %reduce-scatter.11.cloned.1.call-done = f32[96,768]{1,0:T(8,128)} async-done(((f32[3072,768]{1,0:T(8,128)}), f32[96,768]{1,0:T(8,128)}) %reduce-scatter.11.cloned.1.call-update) | async-done | bytes 294928 | tf_op jit(solution)/shard_map/reduce_scatter | solution.py:263
  986.9 142.1 %reduce-scatter.9.cloned.1.call-done = f32[24,3072]{1,0:T(8,128)} async-done(((f32[768,3072]{1,0:T(8,128)}), f32[24,3072]{1,0:T(8,128)}) %reduce-scatter.9.cloned.1.call-update) | async-done | bytes 294928 | tf_op jit(solution)/shard_map/reduce_scatter | solution.py:261
  (572 shorter events, 453.9 us)
Async XLA Ops:
  7.2 53.6 %copy-start.4 = (bf16[1024,768]{1,0:T(8,128)(2,1)S(1)}, bf16[1024,768]{1,0:T(8,128)(2,1)}, u32[]{:S(2)}) copy-start(bf16[1024,768]{1,0:T(8,128)(2,1)} %param.22) | copy-start | bytes 4718596
  7.2 66.5 %all-gather.5.cloned.1.call-start = ((), (), s32[]{:S(2)}) async-start(), calls=%async_computation.4 | async-start | bytes 3649536 | tf_op jit(solution)/shard_map/all_gather | solution.py:87
  7.9 319.2 %all-gather.7.cloned.1.call-start = ((), (), s32[]{:S(2)}) async-start(), calls=%async_computation.5 | async-start | bytes 1216512 | tf_op jit(solution)/shard_map/all_gather | solution.py:88
  8.7 323.3 %all-gather.11.cloned.1.call-start = ((), (), s32[]{:S(2)}) async-start(), calls=%async_computation.7 | async-start | bytes 4866048 | tf_op jit(solution)/shard_map/all_gather | solution.py:92
  9.4 322.6 %all-gather.9.cloned.1.call-start = ((), (), s32[]{:S(2)}) async-start(), calls=%async_computation.6 | async-start | bytes 4866048 | tf_op jit(solution)/shard_map/all_gather | solution.py:90
  10.0 799.0 %reduce-scatter.7.cloned.1.call-start = ((), (), s32[]{:S(2)}) async-start(), calls=%async_computation.9 | async-start | bytes 2433024 | tf_op jit(solution)/shard_map/reduce_scatter | solution.py:259
  59.0 2.4 copy-start.10
  59.0 22.6 %copy-start.7 = (bf16[3072]{0:T(1024)(128)(2,1)}, bf16[3072]{0:T(1024)(128)(2,1)S(1)}, u32[]{:S(2)}) copy-start(bf16[3072]{0:T(1024)(128)(2,1)S(1)} %get-tuple-element.836) | copy-start | bytes 18436
  59.0 22.6 %copy-start.12 = (bf16[768]{0:T(1024)(128)(2,1)}, bf16[768]{0:T(1024)(128)(2,1)S(1)}, u32[]{:S(2)}) copy-start(bf16[768]{0:T(1024)(128)(2,1)S(1)} %get-tuple-element.834) | copy-start | bytes 4612
  59.0 22.6 %copy-start.17 = (f32[768]{0:T(1024)}, f32[768]{0:T(1024)S(1)}, u32[]{:S(2)}) copy-start(f32[768]{0:T(1024)S(1)} %convert_element_type.134) | copy-start | bytes 9220
  59.1 22.6 %copy-start.24 = (f32[768]{0:T(1024)}, f32[768]{0:T(1024)S(1)}, u32[]{:S(2)}) copy-start(f32[768]{0:T(1024)S(1)} %convert_element_type.135) | copy-start | bytes 9220
  60.8 20.9 %copy-start.14 = (f32[1024]{0:T(1024)}, f32[1024]{0:T(1024)S(1)}, u32[]{:S(2)}) copy-start(f32[1024]{0:T(1024)S(1)} %broadcast_multiply_fusion.2) | copy-start | bytes 12292
  61.4 20.3 %copy-start.21 = (f32[1024]{0:T(1024)}, f32[1024]{0:T(1024)S(1)}, u32[]{:S(2)}) copy-start(f32[1024]{0:T(1024)S(1)} %fusion.111) | copy-start | bytes 12292
  61.4 20.2 %copy-start.19 = (f32[1024]{0:T(1024)}, f32[1024]{0:T(1024)S(1)}, u32[]{:S(2)}) copy-start(f32[1024]{0:T(1024)S(1)} %fusion.113) | copy-start | bytes 12292
  103.3 4.5 copy-start.23
  103.3 4.5 copy-start.27
  109.9 2.0 copy-start
  119.1 2.0 copy-start
  128.3 2.0 copy-start
  137.4 2.0 copy-start
  146.5 2.0 copy-start
  155.6 2.0 copy-start
  164.8 2.0 copy-start
  173.9 2.1 copy-start
  183.1 2.0 copy-start
  192.3 2.0 copy-start
  201.4 2.0 copy-start
  210.5 2.0 copy-start
  228.8 2.0 copy-start
  237.9 2.0 copy-start
  247.0 2.0 copy-start
  256.2 2.0 copy-start
  265.3 2.0 copy-start
  274.4 2.0 copy-start
  332.3 6.6 slice-start
  334.0 4.9 copy-start.2
  334.0 4.9 slice-start.1
  334.1 11.5 %slice-start.2 = ((s8[4718592]{0:T(1024)(128)(4,1)}), s8[4194304]{0:T(1024)(128)(4,1)S(1)}, s32[]{:S(2)}) async-start(s8[4718592]{0:T(1024)(128)(4,1)} %bitcast.247), calls=%async_computation.14 | async-start | bytes 8388608 | tf_op jit(solution)/shard_map/while
  338.9 6.6 copy-start.29
  339.0 6.6 slice-start.3
  345.6 3.0 copy-start.1
  350.6 7.4 copy-start.3
  368.5 6.6 slice-start
  370.1 4.9 copy-start.2
  370.2 4.9 slice-start.1
  370.2 11.5 %slice-start.2 = ((s8[4718592]{0:T(1024)(128)(4,1)}), s8[4194304]{0:T(1024)(128)(4,1)S(1)}, s32[]{:S(2)}) async-start(s8[4718592]{0:T(1024)(128)(4,1)} %bitcast.247), calls=%async_computation.14 | async-start | bytes 8388608 | tf_op jit(solution)/shard_map/while
  375.0 6.6 copy-start.29
  375.1 6.6 slice-start.3
  381.7 3.0 copy-start.1
  386.8 8.8 copy-start.3
  408.9 4.6 copy-start.26
  427.1 418.4 %reduce-scatter.5.cloned.1.call-start = ((), (), s32[]{:S(2)}) async-start(), calls=%async_computation.8 | async-start | bytes 7299072 | tf_op jit(solution)/shard_map/reduce_scatter | solution.py:258
  427.1 289.6 %copy-start.15 = (f32[1024]{0:T(1024)S(1)}, f32[1024]{0:T(1024)}, u32[]{:S(2)}) copy-start(f32[1024]{0:T(1024)} %copy-done.14) | copy-start | bytes 12292
  427.1 289.6 %copy-start.18 = (f32[768]{0:T(1024)S(1)}, f32[768]{0:T(1024)}, u32[]{:S(2)}) copy-start(f32[768]{0:T(1024)} %copy-done.17) | copy-start | bytes 9220
  427.1 289.6 %copy-start.20 = (f32[1024]{0:T(1024)S(1)}, f32[1024]{0:T(1024)}, u32[]{:S(2)}) copy-start(f32[1024]{0:T(1024)} %copy-done.19) | copy-start | bytes 12292
  427.1 289.6 %copy-start.25 = (f32[768]{0:T(1024)S(1)}, f32[768]{0:T(1024)}, u32[]{:S(2)}) copy-start(f32[768]{0:T(1024)} %copy-done.24) | copy-start | bytes 9220
  726.8 260.1 %reduce-scatter.11.cloned.1.call-start = ((), (), s32[]{:S(2)}) async-start(), calls=%async_computation.11 | async-start | bytes 9732096 | tf_op jit(solution)/shard_map/reduce_scatter | solution.py:263
  727.6 401.4 %reduce-scatter.9.cloned.1.call-start = ((), (), s32[]{:S(2)}) async-start(), calls=%async_computation.10 | async-start | bytes 9732096 | tf_op jit(solution)/shard_map/reduce_scatter | solution.py:261
  728.4 8.7 copy-start.22
  728.4 8.7 copy-start.5
  782.3 5.1 copy-start.8
  782.3 5.1 copy-start.11
  782.3 5.1 copy-start.13
  782.3 5.1 copy-start.16
  (9 other events, 15.3 us)
Sparse Core Ops, SparseCore 0:
  10.8 62.8 all-gather.4
  76.5 52.8 all-gather.6
  132.2 62.4 all-gather.10
  197.4 62.4 all-gather.8
  427.2 98.3 reduce-scatter.6
  726.9 118.4 reduce-scatter.4
  851.9 134.9 reduce-scatter.10
  994.4 134.5 reduce-scatter.8
where the time goes:
time: 1150 us; the launch traced here: 1140 us
  matrix products  456 us (40%)
  waiting for transfers between devices  336 us (29%)
  local copies, waits for them, and re-layouts  161 us (14%)
  other arithmetic  82.5 us (7%)
  blocking collectives  82.4 us (7%)
  between operations  15.1 us (1%)
    reduce_scatter x1, waiting for transfers between devices, body(): lax.psum_scatter(grad_expand, ('dp', 'fsdp'), scatter_dimension=0, tiled=...  142 us
    reduce_scatter x1, waiting for transfers between devices, body(): lax.psum_scatter(grad_reduce, ('dp', 'fsdp'), scatter_dimension=0, tiled=...  141 us
    dot_general x48, matrix products, masked_scores(): jnp.einsum('qe,ke->qk', queries, key_rows, preferred_element_type=jnp.flo...  99.1 us
    unnamed x2, blocking collectives  82.4 us
    dot_general x24, matrix products, attend_forward(): jnp.einsum('qk,ke->qe', probability, value_rows, preferred_element_type=j...  73.2 us
    while x80, local copies, waits for them, and re-layouts  47 us
    dot_general x24, matrix products, attend_backward(): jnp.einsum('qe,ke->qk', grad_out, value_rows, preferred_element_type=jnp....  42.2 us
    dot_general x24, matrix products, attend_backward(): jnp.einsum('qk,qe->ke', probability.astype(jnp.bfloat16), grad_out, prefe...  40.3 us
  transfers between devices with their start and end apart: 8, of which 4 were waited for; matrix products, arithmetic and copies ran while one was open for 49% of the time, Pallas kernels for 0%

commit v1 on v0

v1 whole, which is shorter than its diff:
```python
import functools
import math

import jax
import jax.numpy as jnp
from jax import lax
from jax.experimental import pallas as pl
from jax.experimental.pallas import tpu as pltpu
from jax.sharding import PartitionSpec as P

D = 768
HD = 32
HEADS = 24
WIN = 1024
BLOCK = 256
EPS = 1e-05
LOG2E = math.log2(math.e)
BIG = float(2**30)
VEC = 128
f32 = jnp.float32
bf16 = jnp.bfloat16
VMEM_LIMIT = 58 << 20
NN = (((1,), (0,)), ((), ()))
NT = (((1,), (1,)), ((), ()))
ANY = pl.BlockSpec(memory_space=pl.ANY)
SMEM = pl.BlockSpec(memory_space=pltpu.SMEM)
PARAMS = pltpu.CompilerParams(vmem_limit_bytes=VMEM_LIMIT)


def dot(a, b, dims=NN):
    return lax.dot_general(a, b, dims, preferred_element_type=f32)


def whole(shape):
    return pl.BlockSpec(shape, lambda *_: (0,) * len(shape))


def flip(value, bit, count):
    return lax.ppermute(value, "dp", [(i, i ^ bit) for i in range(count)])


def shift(value, step, count):
    return lax.ppermute(value, "fsdp", [(i, (i + step) % count) for i in range(count)])


def gather_z(shard, nf):
    parts = [shard] + [shift(shard, k, nf) for k in range(1, nf)]
    me = lax.axis_index("fsdp")
    slots = [lax.select_n(lax.rem(me - j + nf, nf), *parts) for j in range(nf)]
    return jnp.concatenate(slots, axis=0)


def gather_dp(block, order, nd):
    blocks = {0: block}
    for bit in order:
        for m in list(blocks):
            blocks[m ^ bit] = flip(blocks[m], bit, nd)
    return [blocks[m] for m in range(nd)]


def orders(nd):
    upper = [1 << i for i in range(1, nd.bit_length() - 1)]
    return upper, upper[::-1]


def add(a, b):
    return (a.astype(f32) + b.astype(f32)).astype(bf16)


def scatter_dp(send, keep, order, nd):
    got = flip(send, 1, nd)
    masks = list(range(nd // 2))
    total = add(keep, got)
    for bit in order:
        half = bit >> 1
        low = [i for i, m in enumerate(masks) if not m & half]
        high = [i for i, m in enumerate(masks) if m & half]
        out = jnp.stack([total[i] for i in high])
        stay = jnp.stack([total[i] for i in low])
        total = add(stay, flip(out, bit, nd))
        masks = [masks[i] for i in low]
    return total[0]


def scatter_z(block, rows, nf):
    me = lax.axis_index("fsdp")

    def piece(z):
        got, at = [], 0
        for r in rows:
            got.append(lax.dynamic_slice_in_dim(block, at + z * r, r, 0))
            at += nf * r
        return got[0] if len(got) == 1 else jnp.concatenate(got, axis=0)

    total = piece(me).astype(f32)
    for k in range(1, nf):
        total = total + shift(piece(lax.rem(me + k, nf)), k, nf).astype(f32)
    return total


def load_blocks(me, refs, target, sems, base):
    rows = refs[0].shape[0]
    copies = []
    for m, ref in enumerate(refs):
        at = pl.multiple_of((me ^ m) * rows, 16)
        copy = pltpu.make_async_copy(ref, target.at[pl.ds(at, rows), :], sems.at[base + m])
        copy.start()
        copies.append(copy)
    return copies


def norm_parts(v):
    c = v - jnp.mean(v, axis=-1, keepdims=True)
    rstd = lax.rsqrt(jnp.mean(c * c, axis=-1, keepdims=True) + EPS)
    return c * rstd, rstd


def norm_back(grad, gain, h, rstd):
    e = grad * gain
    return (e - jnp.mean(e, -1, keepdims=True) - h * jnp.mean(e * h, -1, keepdims=True)) * rstd


def project_kernel(nd, me_ref, x_ref, *rest):
    w1, w2 = rest[:nd], rest[nd : 2 * nd]
    pt_ref, nt_ref, vec_ref, s1, s2, sems = rest[2 * nd :]
    me = me_ref[0]
    first = load_blocks(me, w1, s1, sems, 0)
    second = load_blocks(me, w2, s2, sems, nd)
    x = x_ref[...].astype(f32)
    h, _ = norm_parts(x)
    for copy in first:
        copy.wait()
    vec = s1[:, 2 * D : 2 * D + VEC].astype(f32).T
    vec_ref[...] = vec[:16]
    normed = (h * vec[0:1] + vec[1:2]).astype(bf16)
    nt_ref[...] = normed.T
    for c in range(0, 2 * D, BLOCK):
        pt_ref[c : c + BLOCK, :] = dot(s1[:, c : c + BLOCK].T, nt_ref[...]).astype(bf16)
    for copy in second:
        copy.wait()
    for c in range(0, D, BLOCK):
        pt_ref[2 * D + c : 2 * D + c + BLOCK, :] = dot(
            s2[:, c : c + BLOCK].T, nt_ref[...]
        ).astype(bf16)


def project(me, tokens, w1, w2):
    nd = len(w1)
    return pl.pallas_call(
        functools.partial(project_kernel, nd),
        in_specs=[SMEM, whole((WIN, D))] + [ANY] * (2 * nd),
        out_specs=[whole((3 * D, WIN)), whole((D, WIN)), whole((16, D))],
        out_shape=[
            jax.ShapeDtypeStruct((3 * D, WIN), bf16),
            jax.ShapeDtypeStruct((D, WIN), bf16),
            jax.ShapeDtypeStruct((16, D), f32),
        ],
        scratch_shapes=[
            pltpu.VMEM((D, w1[0].shape[1]), bf16),
            pltpu.VMEM((D, w2[0].shape[1]), bf16),
            pltpu.SemaphoreType.DMA((2 * nd,)),
        ],
        grid=(1,),
        compiler_params=PARAMS,
        cost_estimate=pl.CostEstimate(flops=2 * WIN * D * 3 * D, bytes_accessed=12 << 20, transcendentals=0),
        name="project",
    )(me, tokens, *w1, *w2)


GH = 8
SH = 8
GR = GH * HD


def causal_penalty():
    ik = lax.broadcasted_iota(jnp.int32, (BLOCK, BLOCK), 0)
    iq = lax.broadcasted_iota(jnp.int32, (BLOCK, BLOCK), 1)
    return jnp.where(iq >= ik, 0.0, -BIG)


def split_scaled(q):
    scaled = q.astype(f32) * (HD**-0.5 * LOG2E)
    high = scaled.astype(bf16)
    return high, (scaled - high.astype(f32)).astype(bf16)


def episode_rows(seg):
    hot = lax.broadcasted_iota(jnp.int32, (8, WIN), 0) == seg
    return hot.astype(f32), jnp.where(hot, 0.0, -BIG)


def attend_kernel(q_ref, k_ref, v_ref, seg_ref, out_ref, lse_ref, qa, ka, va, cm):
    @pl.when(pl.program_id(0) == 0)
    def _():
        cm[...] = causal_penalty()

    hot, pen = episode_rows(seg_ref[...])
    pad = jnp.zeros((56, WIN), f32)
    tail_q = jnp.concatenate([hot, pad], axis=0).astype(bf16)
    tail_k = jnp.concatenate([pen, pad], axis=0).astype(bf16)
    ones = jnp.ones((16, WIN), bf16)
    for h in range(GH):
        rows = slice(h * HD, (h + 1) * HD)
        high, low = split_scaled(q_ref[rows, :])
        k = k_ref[rows, :]
        qa[h] = jnp.concatenate([high, low, tail_q], axis=0)
        ka[h] = jnp.concatenate([k, k, tail_k], axis=0).T
        va[h] = jnp.concatenate([v_ref[rows, :], ones], axis=0)
    c = cm[...]
    for qb in range(WIN // BLOCK):
        k0, k1 = max(0, qb - 2) * BLOCK, (qb + 1) * BLOCK
        qs = slice(qb * BLOCK, k1)
        for hb in range(0, GH, SH):
            heads = range(hb, hb + SH)
            s = [dot(ka[h, k0:k1, :], qa[h, :, qs]) for h in heads]
            w = k1 - k0 - BLOCK
            s = [jnp.concatenate([x[:w], x[w:] + c], axis=0) if w else x + c for x in s]
            top = [jnp.max(x, axis=0, keepdims=True) for x in s]
            p = [jnp.exp2(x - y) for x, y in zip(s, top)]
            o = [dot(va[h, :, k0:k1], y.astype(bf16)) for h, y in zip(heads, p)]
            for i, h in enumerate(heads):
                total = o[i][HD : HD + 1]
                out_ref[h * HD : (h + 1) * HD, qs] = (o[i][:HD] * (1.0 / total)).astype(bf16)
                lse_ref[h, :, qs] = top[i] + jnp.log2(total)


def head_rows(offset):
    return pl.BlockSpec((GR, WIN), lambda g: (g + offset, 0))


def attend(project_t, seg):
    groups = HEADS // GH
    return pl.pallas_call(
        attend_kernel,
        grid=(groups,),
        in_specs=[head_rows(0), head_rows(groups), head_rows(2 * groups), whole((1, WIN))],
        out_specs=[head_rows(0), pl.BlockSpec((GH, 1, WIN), lambda g: (g, 0, 0))],
        out_shape=[
            jax.ShapeDtypeStruct((D, WIN), bf16),
            jax.ShapeDtypeStruct((HEADS, 1, WIN), f32),
        ],
        scratch_shapes=[
            pltpu.VMEM((GH, 128, WIN), bf16),
            pltpu.VMEM((GH, WIN, 128), bf16),
            pltpu.VMEM((GH, HD + 16, WIN), bf16),
            pltpu.VMEM((BLOCK, BLOCK), f32),
        ],
        compiler_params=PARAMS,
        cost_estimate=pl.CostEstimate(flops=20_000_000_000, bytes_accessed=8 << 20, transcendentals=0),
        name="attend",
    )(project_t, project_t, project_t, seg)


def attend_back_kernel(
    q_ref, k_ref, v_ref, o_ref, do_ref, lse_ref, seg_ref, dq_ref, dk_ref, dv_ref, qa, ka, va, da, aq, cm
):
    @pl.when(pl.program_id(0) == 0)
    def _():
        cm[...] = causal_penalty()

    hot, pen = episode_rows(seg_ref[...])
    ids = lax.broadcasted_iota(jnp.int32, (8, WIN), 0)
    ones3 = jnp.where(ids < 3, 1.0, 0.0)
    z48 = jnp.zeros((48, WIN), f32)
    z88 = jnp.zeros((88, WIN), f32)

    def rows3(v):
        a = v.astype(bf16).astype(f32)
        b = (v - a).astype(bf16).astype(f32)
        return jnp.where(ids == 0, a, jnp.where(ids == 1, b, jnp.where(ids == 2, v - a - b, 0.0)))

    tail_k = jnp.concatenate([pen, ones3, z48], axis=0).astype(bf16)
    tail_v = jnp.concatenate([ones3, z88], axis=0).astype(bf16)
    for h in range(GH):
        rows = slice(h * HD, (h + 1) * HD)
        high, low = split_scaled(q_ref[rows, :])
        k, v, g = k_ref[rows, :], v_ref[rows, :], do_ref[rows, :]
        delta = jnp.sum(g.astype(f32) * o_ref[rows, :].astype(f32), axis=0, keepdims=True)
        tail_q = jnp.concatenate([hot, rows3(-lse_ref[h]), z48], axis=0).astype(bf16)
        tail_g = jnp.concatenate([rows3(-delta), z88], axis=0).astype(bf16)
        qa[h] = jnp.concatenate([high, low, tail_q], axis=0)
        ka[h] = jnp.concatenate([k, k, tail_k], axis=0).T
        va[h] = jnp.concatenate([v, tail_v], axis=0).T
        da[h] = jnp.concatenate([g, tail_g], axis=0)
    c = cm[...]
    scale = HD**-0.5
    step = 4
    nb = WIN // BLOCK
    for kb in range(nb):
        q0, q1 = kb * BLOCK, min(nb, kb + 3) * BLOCK
        ks = slice(q0, q0 + BLOCK)
        for hb in range(0, GH, step):
            heads = range(hb, hb + step)
            rows = [slice(h * HD, (h + 1) * HD) for h in heads]
            s = [dot(ka[h, ks, :], qa[h, :, q0:q1]) for h in heads]
            dp = [dot(va[h, ks, :], da[h, :, q0:q1]) for h in heads]
            s = [
                jnp.concatenate([x[:, :BLOCK] + c, x[:, BLOCK:]], axis=1) if q1 - q0 > BLOCK else x + c
                for x in s
            ]
            p = [jnp.exp2(x) for x in s]
            ds = [(x * y).astype(bf16) for x, y in zip(p, dp)]
            pb = [x.astype(bf16) for x in p]
            dv = [dot(do_ref[x, q0:q1], y, NT) for x, y in zip(rows, pb)]
            dk = [dot(q_ref[x, q0:q1], y, NT) for x, y in zip(rows, ds)]
            dq = [dot(k_ref[x, ks], y) for x, y in zip(rows, ds)]
            for i in range(step):
                dv_ref[rows[i], ks] = dv[i].astype(bf16)
                dk_ref[rows[i], ks] = (dk[i] * scale).astype(bf16)
                done = min(nb, kb + 2) * BLOCK if kb else 0
                if done > q0:
                    aq[rows[i], q0:done] += dq[i][:, : done - q0]
                if q1 > max(done, q0):
                    at = max(done, q0)
                    aq[rows[i], at:q1] = dq[i][:, at - q0 :]
    dq_ref[...] = (aq[...] * scale).astype(bf16)


def attend_back(project_t, attended_t, grad_t, lse, seg):
    groups = HEADS // GH
    return pl.pallas_call(
        attend_back_kernel,
        grid=(groups,),
        in_specs=[
            head_rows(0),
            head_rows(groups),
            head_rows(2 * groups),
            head_rows(0),
            head_rows(0),
            pl.BlockSpec((GH, 1, WIN), lambda g: (g, 0, 0)),
            whole((1, WIN)),
        ],
        out_specs=[head_rows(0)] * 3,
        out_shape=[jax.ShapeDtypeStruct((D, WIN), bf16)] * 3,
        scratch_shapes=[
            pltpu.VMEM((GH, 128, WIN), bf16),
            pltpu.VMEM((GH, WIN, 128), bf16),
            pltpu.VMEM((GH, WIN, 128), bf16),
            pltpu.VMEM((GH, 128, WIN), bf16),
            pltpu.VMEM((GR, WIN), f32),
            pltpu.VMEM((BLOCK, BLOCK), f32),
        ],
        compiler_params=PARAMS,
        cost_estimate=pl.CostEstimate(flops=40_000_000_000, bytes_accessed=14 << 20, transcendentals=0),
        name="attend_back",
    )(project_t, project_t, project_t, attended_t, grad_t, lse, seg)


def gelu_both(u):
    a, b = math.sqrt(2 / math.pi), 0.044715
    sq = u * u
    t = jnp.tanh(u * (a + (a * b) * sq))
    half = 0.5 + 0.5 * t
    slope = half + (0.5 * u) * (1.0 - t * t) * (a + (3 * a * b) * sq)
    return u * half, slope


def ffn_kernel(nd, me_ref, x_ref, at_ref, cot_ref, vec_ref, be_ref, *rest):
    w2, we, wr = rest[:nd], rest[nd : 2 * nd], rest[2 * nd : 3 * nd]
    (
        out_ref, gm_ref, dt_ref, es_ref, ek_ref, rs_ref, rk_ref, gbe_ref, gv_ref,
        comb, exp, red, mid, n2, n2t, cott, oacc, nacc, ascr, gscr, ext, rdt, tmp, sems,
    ) = rest[3 * nd :]
    i = pl.program_id(0)
    steps = nd // 2
    me = me_ref[0]
    core = me & 1
    chunk = exp.shape[1] // steps
    rb = D // nd
    rr = chunk // 2
    tb = 256

    @pl.when(i == 0)
    def _():
        got = load_blocks(me, [r.at[:, D : 2 * D] for r in w2], comb, sems, 0)
        late = load_blocks(me, we, exp, sems, nd) + load_blocks(me, wr, red, sems, 2 * nd)
        cott[...] = cot_ref[...].T
        for copy in got:
            copy.wait()
        for t in range(0, WIN, tb):
            rows = slice(t, t + tb)
            m = (
                x_ref[rows, :].astype(f32)
                + dot(at_ref[:, rows].T, comb[...])
                + vec_ref[2:3, :]
            )
            mid[rows, :] = m
            h, _ = norm_parts(m)
            n = (h * vec_ref[3:4, :] + vec_ref[4:5, :]).astype(bf16)
            n2[rows, :] = n
            n2t[:, rows] = n.T
        oacc[...] = jnp.zeros_like(oacc)
        nacc[...] = jnp.zeros_like(nacc)
        for copy in late:
            copy.wait()

    j = (me >> 1) ^ i
    cols = pl.ds(pl.multiple_of(j * chunk, 128), chunk)
    ext[...] = exp[:, cols].T
    rdt[...] = red[cols, :].T
    bias = be_ref[...]
    gb = jnp.zeros((1, chunk), f32)
    for t in range(0, WIN, tb):
        rows = slice(t, t + tb)
        u = dot(n2[rows, :], exp[:, cols]) + bias
        ga = dot(cot_ref[rows, :], rdt[...])
        act, slope = gelu_both(u)
        act = act.astype(bf16)
        gu = (ga * slope).astype(bf16)
        ascr[rows, :] = act
        gscr[rows, :] = gu
        gb = gb + jnp.sum(gu.astype(f32), axis=0, keepdims=True)
        oacc[rows, :] += dot(act, red[cols, :])
        nacc[rows, :] += dot(gu, ext[...])
    gbe_ref[...] = gb
    ge = dot(n2t[...], gscr[...]).astype(bf16)
    tmp[...] = ge
    for s in range(steps):
        far = pl.multiple_of((me ^ (2 * s + 1)) * rb, 16)
        near = pl.multiple_of((me ^ (2 * s)) * rb, 16)
        es_ref[s] = tmp[pl.ds(far, rb), :]
        ek_ref[s] = tmp[pl.ds(near, rb), :]
    gr = dot(cott[...], ascr[...]).astype(bf16)
    ext[...] = gr.T
    rs_ref[i, :rr, :] = ext[pl.ds(pl.multiple_of((1 - core) * rr, 16), rr), :]
    rk_ref[i, :rr, :] = ext[pl.ds(pl.multiple_of(core * rr, 16), rr), :]

    @pl.when(i == steps - 1)
    def _():
        zero = jnp.zeros((1, D), f32)
        ggain, gshift, gattend, greduce = zero, zero, zero, zero
        for t in range(0, WIN, tb):
            rows = slice(t, t + tb)
            m = mid[rows, :]
            out_ref[rows, :] = (m + oacc[rows, :] + vec_ref[5:6, :]).astype(bf16)
            h, rstd = norm_parts(m)
            g = nacc[rows, :]
            cot = cot_ref[rows, :].astype(f32)
            gm = cot + norm_back(g, vec_ref[3:4, :], h, rstd)
            gm_ref[rows, :] = gm
            low = gm.astype(bf16)
            n2[rows, :] = low
            n2t[:, rows] = low.T
            ggain += jnp.sum(g * h, axis=0, keepdims=True)
            gshift += jnp.sum(g, axis=0, keepdims=True)
            gattend += jnp.sum(low.astype(f32), axis=0, keepdims=True)
            greduce += jnp.sum(cot, axis=0, keepdims=True)
        gv_ref[...] = jnp.concatenate(
            [zero, zero, gattend, ggain, gshift, greduce, zero, zero], axis=0
        )
        dt_ref[...] = dot(comb[...], n2t[...]).astype(bf16)
        mid[:D, :] = dot(at_ref[...], n2[...])
        for s in range(steps):
            far = pl.multiple_of((me ^ (2 * s + 1)) * rb, 16)
            near = pl.multiple_of((me ^ (2 * s)) * rb, 16)
            rs_ref[s, rr : rr + rb, :] = mid[pl.ds(far, rb), :].astype(bf16)
            rk_ref[s, rr : rr + rb, :] = mid[pl.ds(near, rb), :].astype(bf16)


def feed_forward(me, tokens, attended_t, cotangent, vec, bias, w2, we, wr):
    nd = len(we)
    ff = we[0].shape[1]
    steps = nd // 2
    chunk = ff // steps
    rb, rr = D // nd, chunk // 2
    half_e = pl.BlockSpec((steps, rb, chunk), lambda i, s: (0, 0, (s[0] >> 1) ^ i))
    by_chunk = pl.BlockSpec((1, chunk), lambda i, s: (0, (s[0] >> 1) ^ i))
    shape = jax.ShapeDtypeStruct
    return pl.pallas_call(
        functools.partial(ffn_kernel, nd),
        grid_spec=pltpu.PrefetchScalarGridSpec(
            num_scalar_prefetch=1,
            grid=(steps,),
            in_specs=[whole((WIN, D)), whole((D, WIN)), whole((WIN, D)), whole((16, D)), by_chunk]
            + [ANY] * (3 * nd),
            out_specs=[
                whole((WIN, D)),
                whole((WIN, D)),
                whole((D, WIN)),
                half_e,
                half_e,
                whole((steps, rr + rb, D)),
                whole((steps, rr + rb, D)),
                by_chunk,
                whole((8, D)),
            ],
            scratch_shapes=[
                pltpu.VMEM((D, D), bf16),
                pltpu.VMEM((D, ff), bf16),
                pltpu.VMEM((ff, D), bf16),
                pltpu.VMEM((WIN, D), f32),
                pltpu.VMEM((WIN, D), bf16),
                pltpu.VMEM((D, WIN), bf16),
                pltpu.VMEM((D, WIN), bf16),
                pltpu.VMEM((WIN, D), f32),
                pltpu.VMEM((WIN, D), f32),
                pltpu.VMEM((WIN, chunk), bf16),
                pltpu.VMEM((WIN, chunk), bf16),
                pltpu.VMEM((chunk, D), bf16),
                pltpu.VMEM((D, chunk), bf16),
                pltpu.VMEM((D, chunk), bf16),
                pltpu.SemaphoreType.DMA((3 * nd,)),
            ],
        ),
        out_shape=[
            shape((WIN, D), bf16),
            shape((WIN, D), f32),
            shape((D, WIN), bf16),
            shape((steps, rb, ff), bf16),
            shape((steps, rb, ff), bf16),
            shape((steps, rr + rb, D), bf16),
            shape((steps, rr + rb, D), bf16),
            shape((1, ff), f32),
            shape((8, D), f32),
        ],
        compiler_params=PARAMS,
        cost_estimate=pl.CostEstimate(flops=12 * WIN * D * ff, bytes_accessed=40 << 20, transcendentals=0),
        name="feed_forward",
    )(me, tokens, attended_t, cotangent, vec, bias, *w2, *we, *wr)


def project_back_kernel(nd, me_ref, x_ref, gm_ref, nt_ref, dq_ref, dk_ref, dv_ref, vec_ref, gv_ref, *rest):
    w1, w2 = rest[:nd], rest[nd : 2 * nd]
    gt_ref, as_ref, ak_ref, bs_ref, bk_ref, s1, s2, tmp, gx, gvt, sems = rest[2 * nd :]
    me = me_ref[0]
    steps = nd // 2
    rb = D // nd
    first = load_blocks(me, w1, s1, sems, 0)
    second = load_blocks(me, w2, s2, sems, nd)

    def emit(source, send, keep, at, width):
        for s in range(steps):
            far = pl.multiple_of((me ^ (2 * s + 1)) * rb, 16)
            near = pl.multiple_of((me ^ (2 * s)) * rb, 16)
            send[s, :, at : at + width] = source[pl.ds(far, rb), :]
            keep[s, :, at : at + width] = source[pl.ds(near, rb), :]

    for c, (ref, send, keep, at) in enumerate(
        ((dq_ref, as_ref, ak_ref, 0), (dk_ref, as_ref, ak_ref, D), (dv_ref, bs_ref, bk_ref, 0))
    ):
        for b in range(0, D, BLOCK):
            tmp[:, b : b + BLOCK] = dot(nt_ref[...], ref[b : b + BLOCK, :].T).astype(bf16)
        emit(tmp, send, keep, at, D)
    for copy in first:
        copy.wait()
    for copy in second:
        copy.wait()
    for t in range(0, WIN, BLOCK):
        cols = slice(t, t + BLOCK)
        gx[:, cols] = (
            dot(s1[:, :D], dq_ref[:, cols])
            + dot(s1[:, D : 2 * D], dk_ref[:, cols])
            + dot(s2[:, :D], dv_ref[:, cols])
        )
    ggain = jnp.zeros((1, D), f32)
    gshift = jnp.zeros((1, D), f32)
    for t in range(0, WIN, BLOCK):
        rows = slice(t, t + BLOCK)
        g = gx[:, rows].T
        h, rstd = norm_parts(x_ref[rows, :].astype(f32))
        gt_ref[rows, :] = gm_ref[rows, :] + norm_back(g, vec_ref[0:1, :], h, rstd)
        ggain += jnp.sum(g * h, axis=0, keepdims=True)
        gshift += jnp.sum(g, axis=0, keepdims=True)
    rows = jnp.concatenate(
        [ggain, gshift, gv_ref[2:, :], jnp.zeros((VEC - gv_ref.shape[0], D), f32)], axis=0
    )
    gvt[...] = rows.T.astype(bf16)
    emit(gvt, bs_ref, bk_ref, D, VEC)


def project_back(me, tokens, grad_middle, normed_t, dq, dk, dv, vec, gvec, w1, w2):
    nd = len(w1)
    steps, rb = nd // 2, D // nd
    shape = jax.ShapeDtypeStruct
    return pl.pallas_call(
        functools.partial(project_back_kernel, nd),
        grid=(1,),
        in_specs=[SMEM, whole((WIN, D)), whole((WIN, D))]
        + [whole((D, WIN))] * 4
        + [whole((16, D)), whole((16, D))]
        + [ANY] * (2 * nd),
        out_specs=[whole((WIN, D))]
        + [whole((steps, rb, 2 * D))] * 2
        + [whole((steps, rb, D + VEC))] * 2,
        out_shape=[shape((WIN, D), f32)]
        + [shape((steps, rb, 2 * D), bf16)] * 2
        + [shape((steps, rb, D + VEC), bf16)] * 2,
        scratch_shapes=[
            pltpu.VMEM((D, w1[0].shape[1]), bf16),
            pltpu.VMEM((D, w2[0].shape[1]), bf16),
            pltpu.VMEM((D, D), bf16),
            pltpu.VMEM((D, WIN), f32),
            pltpu.VMEM((D, VEC), bf16),
            pltpu.SemaphoreType.DMA((2 * nd,)),
        ],
        compiler_params=PARAMS,
        cost_estimate=pl.CostEstimate(flops=4 * WIN * D * 3 * D, bytes_accessed=30 << 20, transcendentals=0),
        name="project_back",
    )(me, tokens, grad_middle, normed_t, dq, dk, dv, vec, gvec, *w1, *w2)


def body(nd, nf, tokens, segment_ids, cotangent, projector, combiner, attend_bias, expander,
         expand_bias, reducer, reduce_bias, first_gain, first_shift, second_gain, second_shift):
    r = projector.shape[0]
    up, down = orders(nd)
    me = lax.axis_index("dp").astype(jnp.int32).reshape(1)
    vec = jnp.stack(
        [first_gain, first_shift, attend_bias, second_gain, second_shift, reduce_bias], axis=1
    )
    vec = jnp.concatenate([vec, expand_bias.reshape(r, 4), jnp.zeros((r, VEC - 10), bf16)], axis=1)
    shard1 = jnp.concatenate([projector[:, : 2 * D], vec], axis=1)
    shard2 = jnp.concatenate([projector[:, 2 * D :], combiner], axis=1)
    z1, z2 = gather_z(shard1, nf), gather_z(shard2, nf)
    w1, w2 = gather_dp(z1, up + [1], nd), gather_dp(z2, down + [1], nd)
    ze, zr = gather_z(expander, nf), gather_z(reducer, nf)
    we, wr = gather_dp(ze, up + [1], nd), gather_dp(zr, down + [1], nd)

    project_t, normed_t, vecs = project(me, tokens, w1, w2)
    attended_t, lse = attend(project_t, segment_ids)
    bias = vecs[6:10].T.reshape(1, -1)
    out, grad_middle, grad_t, es, ek, rs, rk, gbe, gvec = feed_forward(
        me, tokens, attended_t, cotangent, vecs, bias, w2, we, wr
    )
    ve = scatter_dp(es, ek, up, nd)
    vr = scatter_dp(rs, rk, down, nd)
    grad_expander = scatter_z(ve, [r], nf)
    grad_rc = scatter_z(vr, [reducer.shape[0], r], nf)
    dq, dk, dv = attend_back(project_t, attended_t, grad_t, lse, segment_ids)
    gvec = jnp.concatenate(
        [gvec[:6], gbe.reshape(-1, 4).T, jnp.zeros((6, D), f32)], axis=0
    )
    grad_tokens, s1, k1, s2, k2 = project_back(
        me, tokens, grad_middle, normed_t, dq, dk, dv, vecs, gvec, w1, w2
    )
    g1 = scatter_z(scatter_dp(s1, k1, up, nd), [r], nf)
    g2 = scatter_z(scatter_dp(s2, k2, down, nd), [r], nf)
    small = g2[:, D : D + 10]
    return (
        out,
        grad_tokens,
        jnp.concatenate([g1, g2[:, :D]], axis=1),
        grad_rc[reducer.shape[0] :],
        small[:, 2],
        grad_expander,
        small[:, 6:10].reshape(-1),
        grad_rc[: reducer.shape[0]],
        small[:, 5],
        small[:, 0],
        small[:, 1],
        small[:, 3],
        small[:, 4],
    )


def solution(mesh):
    rows, flat = P(("dp", "fsdp"), None), P(("dp", "fsdp"))
    return jax.shard_map(
        functools.partial(body, mesh.shape["dp"], mesh.shape["fsdp"]),
        mesh=mesh,
        in_specs=(rows, rows, rows, rows, rows, flat, rows, flat, rows, flat, flat, flat, flat, flat),
        out_specs=(rows, rows, rows, rows, flat, rows, flat, rows, flat, flat, flat, flat, flat),
        check_vma=False,
    )
```

time: 1150 us -> 384 us (0.33); the launches traced: 1140 us -> 383 us
  matrix products: 456 us -> 0 us
  waiting for transfers between devices: 336 us -> 129 us
  Pallas kernels: 0 us -> 151 us
  local copies, waits for them, and re-layouts: 161 us -> 20.3 us
  blocking collectives: 82.4 us -> 0 us
  other arithmetic: 82.5 us -> 15.8 us
  starting transfers between devices: 0.56 us -> 65.2 us
  between operations: 15.1 us -> 1.56 us
    dot_general x186 -> x0, matrix products: 456 us -> none  [the longest x48 99.1 us: masked_scores(): jnp.einsum('qe,ke->qk', queries, key_rows, preferred_element_type=jnp.flo...]
    reduce_scatter x4 -> x0, waiting for transfers between devices: 320 us -> none  [the longest x1 142 us: body(): lax.psum_scatter(grad_expand, ('dp', 'fsdp'), scatter_dimension=0, tiled=...]
    pallas_call x0 -> x5, Pallas kernels: none -> 151 us  [the longest x1 51.4 us: feed_forward(): pl.pallas_call(functools.partial(ffn_kernel, nd), grid_spec=pltpu.Prefetc...]
    ppermute x0 -> x64, waiting for transfers between devices: none -> 129 us  [the longest x40 95.2 us: flip(): return lax.ppermute(value, 'dp', [(i, i ^ bit) for i in range(count)])]
    unnamed x2 -> x0, blocking collectives: 82.4 us -> none
    ppermute x0 -> x64, starting transfers between devices: none -> 65.2 us  [the longest x24 40.8 us: shift(): lax.ppermute(value, 'fsdp', [(i, (i + step) % count) for i in range(count)])]
    while x83 -> x0, local copies, waits for them, and re-layouts: 62.2 us -> none
    dynamic_slice x72 -> x5, local copies, waits for them, and re-layouts: 36.9 us -> 0.79 us  [piece(): got.append(lax.dynamic_slice_in_dim(block, at + z * r, r, 0))]
  transfers between devices with their start and end apart: 8 -> 64, of which waited for: 4 -> 27; matrix products, arithmetic and copies ran while one was open for 49% -> 7% of each run, Pallas kernels for 0% -> 12%
where the time goes in v1:
time: 384 us; the launch traced here: 383 us
  Pallas kernels  151 us (39%)
  waiting for transfers between devices  129 us (34%)
  starting transfers between devices  65.2 us (17%)
  local copies, waits for them, and re-layouts  20.3 us (5%)
  other arithmetic  15.8 us (4%)
    ppermute x40, waiting for transfers between devices, flip(): return lax.ppermute(value, 'dp', [(i, i ^ bit) for i in range(count)])  95.2 us
    pallas_call x1, Pallas kernels, feed_forward(): pl.pallas_call(functools.partial(ffn_kernel, nd), grid_spec=pltpu.Prefetc...  51.4 us
    ppermute x24, starting transfers between devices, shift(): lax.ppermute(value, 'fsdp', [(i, (i + step) % count) for i in range(count)])  40.8 us
    pallas_call x1, Pallas kernels, attend_back(): pl.pallas_call(attend_back_kernel, grid=(groups,), in_specs=[head_rows(0)...  39.5 us
    pallas_call x1, Pallas kernels, attend(): pl.pallas_call(attend_kernel, grid=(groups,), in_specs=[head_rows(0), hea...  34.9 us
    ppermute x24, waiting for transfers between devices, shift(): lax.ppermute(value, 'fsdp', [(i, (i + step) % count) for i in range(count)])  33.8 us
    ppermute x40, starting transfers between devices, flip(): return lax.ppermute(value, 'dp', [(i, i ^ bit) for i in range(count)])  24.5 us
    pallas_call x1, Pallas kernels, project_back(): pl.pallas_call(functools.partial(project_back_kernel, nd), grid=(1,), in_...  15.7 us
  transfers between devices with their start and end apart: 64, of which 27 were waited for; matrix products, arithmetic and copies ran while one was open for 7% of the time, Pallas kernels for 12%

profile of v1, /device:TPU:0, one launch (start us, length us, event | category | flops | bytes accessed | tf_op | source)
XLA Modules:
  0.0 383.4 jit_solution(781994693039989081)
XLA Ops:
  2.3 3.0 collective-permute-start.10
  5.3 2.6 collective-permute-start.11
  7.9 1.3 collective-permute-start.12
  9.2 0.9 slice.110
  16.5 2.8 collective-permute-start.2
  20.0 1.5 collective-permute-start.21
  23.2 2.9 collective-permute-start.22
  26.1 2.9 collective-permute-done.1
  29.0 2.5 collective-permute-start.31
  31.6 4.0 %collective-permute-start.32 = (bf16[96,768]{1,0:T(8,128)(2,1)S(1)}, bf16[96,768]{1,0:T(8,128)(2,1)S(1)}, u32[]{:S(2)}, u32[]{:S(2)}) collective-permute-start(bf16[96,768]{1,0:T(8,128)(2,1)S(1)} %copy-done.10), channel_id=1, source_target_pairs={{0,3},{1,0},{2,1},{3,2},{4,7},{5,4},{6,5},{7,6},{8,11},{9,8},{10,9... | collective-permute-start | bytes 442376 | tf_op jit(solution)/shard_map/ppermute | solution.py:43
  35.6 6.1 %collective-permute-done.21 = bf16[24,3072]{1,0:T(8,128)(2,1)S(1)} collective-permute-done((bf16[24,3072]{1,0:T(8,128)(2,1)}, bf16[24,3072]{1,0:T(8,128)(2,1)S(1)}, u32[]{:S(2)}, u32[]{:S(2)}) %collective-permute-start.21) | collective-permute-done | bytes 147488 | tf_op jit(solution)/shard_map/ppermute | solution.py:43
  41.7 1.5 collective-permute-start.16
  43.2 1.5 collective-permute-start.14
  44.8 3.2 collective-permute-done.31
  48.0 1.5 collective-permute-start.4
  49.5 1.5 collective-permute-start.6
  52.7 5.8 %collective-permute-done.4.rest_2_ = bf16[96,1664]{1,0:T(8,128)(2,1)S(1)} collective-permute-done((bf16[96,1664]{1,0:T(8,128)(2,1)S(1)}, bf16[96,1664]{1,0:T(8,128)(2,1)S(1)}, u32[]{:S(2)}, u32[]{:S(2)}) %collective-permute-start.4) | collective-permute-done | bytes 319520 | tf_op jit(solution)/shard_map/ppermute | solution.py:39
  58.5 1.5 collective-permute-start.24
  60.0 1.6 collective-permute-start.8
  61.6 3.2 collective-permute-done.18.rest_14_.rest_6_
  65.6 1.6 collective-permute-start.36
  67.2 3.2 collective-permute-done.8.rest_6_
  70.4 1.5 collective-permute-start.26
  72.5 5.0 %collective-permute-done.24.rest_10_ = bf16[96,3072]{1,0:T(8,128)(2,1)S(1)} collective-permute-done((bf16[96,3072]{1,0:T(8,128)(2,1)S(1)}, bf16[96,3072]{1,0:T(8,128)(2,1)S(1)}, u32[]{:S(2)}, u32[]{:S(2)}) %collective-permute-start.24) | collective-permute-done | bytes 589856 | tf_op jit(solution)/shard_map/ppermute | solution.py:39
  77.5 5.6 %collective-permute-done.36.rest_20_ = bf16[384,768]{1,0:T(8,128)(2,1)S(1)} collective-permute-done((bf16[384,768]{1,0:T(8,128)(2,1)S(1)}, bf16[384,768]{1,0:T(8,128)(2,1)S(1)}, u32[]{:S(2)}, u32[]{:S(2)}) %collective-permute-start.36) | collective-permute-done | bytes 589856 | tf_op jit(solution)/shard_map/ppermute | solution.py:39
  83.1 12.3 %collective-permute-done.26.rest_12_ = bf16[96,3072]{1,0:T(8,128)(2,1)} collective-permute-done((bf16[96,3072]{1,0:T(8,128)(2,1)S(1)}, bf16[96,3072]{1,0:T(8,128)(2,1)}, u32[]{:S(2)}, u32[]{:S(2)}) %collective-permute-start.26) | collective-permute-done | bytes 589856 | tf_op jit(solution)/shard_map/ppermute | solution.py:39
  95.4 1.5 collective-permute-start.28
  98.4 9.9 %project.1 = (bf16[2304,1024]{1,0:T(8,128)(2,1)}, bf16[768,1024]{1,0:T(8,128)(2,1)}, f32[16,768]{1,0:T(8,128)}) custom-call(s32[1]{0:T(128)} %bitcast.me_ref, bf16[1024,768]{1,0:T(8,128)(2,1)} %x_ref.5, bf16[96,1664]{1,0:T(8,128)(2,1)} %copy-done.7, bf16[96,1664]{1,0:T(8,128)(2,1)} %copy-done.19, bf16[96,1664]{1,0:T(8,128)(2,1)} %copy-done.17, ...), custom_call_target="tpu_custom_call" | custom-call | flops 3623878656 | bytes 12582912 | tf_op jit(solution)/shard_map/project/pallas_call | solution.py:149
  109.0 2.2 collective-permute-done.28.rest_14_
  111.2 1.2 collective-permute-done.38.rest_22_
  113.0 34.9 %attend.1 = (bf16[768,1024]{1,0:T(8,128)(2,1)}, f32[24,1,1024]{2,1,0:T(1,128)}) custom-call(bf16[2304,1024]{1,0:T(8,128)(2,1)} %get-tuple-element.35.q_ref.k_ref.v_ref, bf16[2304,1024]{1,0:T(8,128)(2,1)} %get-tuple-element.35.q_ref.k_ref.v_ref, bf16[2304,1024]{1,0:T(8,128)(2,1)} %get-tuple-element.35.q_ref.k_ref.v_ref, s32[1,1024]{1,0:T(1,128)} %seg_ref.3), custom_call_target="tpu_custom_call" | custom-call | flops 20000000000 | bytes 8388608 | tf_op jit(solution)/shard_map/attend/pallas_call | solution.py:233
  150.8 51.4 %feed_forward.1 = (bf16[1024,768]{1,0:T(8,128)(2,1)}, f32[1024,768]{1,0:T(8,128)}, bf16[768,1024]{1,0:T(8,128)(2,1)}, bf16[4,96,3072]{2,1,0:T(8,128)(2,1)}, bf16...) custom-call(s32[1]{0:T(128)} %bitcast.me_ref, ...), custom_call_target="tpu_custom_call" | custom-call | flops 28991029248 | bytes 41943040 | tf_op jit(solution)/shard_map/feed_forward/pallas_call | solution.py:469
  202.7 1.4 reduce.15
  204.7 39.5 %attend_back.1 = (bf16[768,1024]{1,0:T(8,128)(2,1)}, bf16[768,1024]{1,0:T(8,128)(2,1)}, bf16[768,1024]{1,0:T(8,128)(2,1)}) custom-call(bf16[2304,1024]{1,0:T(8,128)(2,1)} %get-tuple-element.35.q_ref.k_ref.v_ref, bf16[2304,1024]{1,0:T(8,128)(2,1)} %get-tuple-element.35.q_ref.k_ref.v_ref, bf16[2304,1024]{1,0:T(8,128)(2,1)} %get-tuple-element.35.q_ref.k_ref.v_ref, ...), custom_call_target="tpu_custom_call" | custom-call | flops 40000000000 | bytes 14680064 | tf_op jit(solution)/shard_map/attend_back/pallas_call | solution.py:321
  244.9 15.7 %project_back.1 = (f32[1024,768]{1,0:T(8,128)}, bf16[4,96,1536]{2,1,0:T(8,128)(2,1)}, bf16[4,96,1536]{2,1,0:T(8,128)(2,1)}, bf16[4,96,896]{2,1,0:T(8,128)(2,1)}, bf16[4,96,896]{2,1,0:T(8,128)(2,1)}) custom-call(s32[1]{0:T(128)} %bitcast.me_ref, bf16[1024,768]{1,0:T(8,128)(2,1)} %x_ref.5, f32[1024,768]{1,0:T(8,128)} %get-tuple-element.39.gm_ref, ...), custom_call_target="tpu_custom_call" | custom-call | flops 7247757312 | bytes 31457280 | tf_op jit(solution)/shard_map/project_back/pallas_call | solution.py:575
  261.2 1.8 collective-permute-done.46
  263.0 1.3 add_convert_fusion.6
  265.6 9.9 %collective-permute-done.47 = bf16[2,96,896]{2,1,0:T(8,128)(2,1)S(1)} collective-permute-done((bf16[2,96,896]{2,1,0:T(8,128)(2,1)}, bf16[2,96,896]{2,1,0:T(8,128)(2,1)S(1)}, u32[]{:S(2)}, u32[]{:S(2)}) %collective-permute-start.47) | collective-permute-done | bytes 344096 | tf_op jit(solution)/shard_map/ppermute | solution.py:39
  277.5 1.5 collective-permute-start.41
  279.0 4.0 %collective-permute-done.48 = bf16[1,96,896]{2,1,0:T(8,128)(2,1)S(1)} collective-permute-done((bf16[1,96,896]{2,1,0:T(8,128)(2,1)S(1)}, bf16[1,96,896]{2,1,0:T(8,128)(2,1)S(1)}, u32[]{:S(2)}, u32[]{:S(2)}) %collective-permute-start.48) | collective-permute-done | bytes 172064 | tf_op jit(solution)/shard_map/ppermute | solution.py:39
  284.4 3.6 collective-permute-start.49
  288.5 1.9 collective-permute-start.51
  291.2 2.1 collective-permute-done.50
  295.5 1.9 slice_reduce_fusion
  297.4 1.2 add_convert_fusion.8
  298.6 1.1 collective-permute-start.42
  299.7 2.6 add_convert_fusion.1
  303.1 2.9 collective-permute-done.42
  306.1 1.5 collective-permute-start.43
  307.6 1.7 collective-permute-start.44
  309.3 1.3 collective-permute-start.45
  312.4 1.7 collective-permute-done.44
  314.6 13.9 %collective-permute-done.59 = bf16[2,96,3072]{2,1,0:T(8,128)(2,1)S(1)} collective-permute-done((bf16[2,96,3072]{2,1,0:T(8,128)(2,1)S(1)}, bf16[2,96,3072]{2,1,0:T(8,128)(2,1)S(1)}, u32[]{:S(2)}, u32[]{:S(2)}) %collective-permute-start.59) | collective-permute-done | bytes 1179680 | tf_op jit(solution)/shard_map/ppermute | solution.py:39
  328.9 1.2 collective-permute-start.60
  330.9 16.0 %collective-permute-done.53 = bf16[2,480,768]{2,1,0:T(8,128)(2,1)S(1)} collective-permute-done((bf16[2,480,768]{2,1,0:T(8,128)(2,1)S(1)}, bf16[2,480,768]{2,1,0:T(8,128)(2,1)S(1)}, u32[]{:S(2)}, u32[]{:S(2)}) %collective-permute-start.53) | collective-permute-done | bytes 1474592 | tf_op jit(solution)/shard_map/ppermute | solution.py:39
  347.5 8.0 %collective-permute-done.60 = bf16[1,96,3072]{2,1,0:T(8,128)(2,1)S(1)} collective-permute-done((bf16[1,96,3072]{2,1,0:T(8,128)(2,1)S(1)}, bf16[1,96,3072]{2,1,0:T(8,128)(2,1)S(1)}, u32[]{:S(2)}, u32[]{:S(2)}) %collective-permute-start.60) | collective-permute-done | bytes 589856 | tf_op jit(solution)/shard_map/ppermute | solution.py:39
  355.8 2.2 collective-permute-start.62
  358.0 1.9 collective-permute-start.63
  360.5 1.5 collective-permute-start.56
  362.1 2.4 collective-permute-done.61
  364.5 1.9 collective-permute-start.57
  366.4 4.3 %collective-permute-done.62 = bf16[24,3072]{1,0:T(8,128)(2,1)S(1)} collective-permute-done((bf16[24,3072]{1,0:T(8,128)(2,1)S(1)}, bf16[24,3072]{1,0:T(8,128)(2,1)S(1)}, u32[]{:S(2)}, u32[]{:S(2)}) %collective-permute-start.62) | collective-permute-done | bytes 147488 | tf_op jit(solution)/shard_map/ppermute | solution.py:43
  371.5 2.3 collective-permute-done.55
  373.8 7.8 %collective-permute-done.56 = bf16[120,768]{1,0:T(8,128)(2,1)S(1)} collective-permute-done((bf16[120,768]{1,0:T(8,128)(2,1)S(1)}, bf16[120,768]{1,0:T(8,128)(2,1)S(1)}, u32[]{:S(2)}, u32[]{:S(2)}) %collective-permute-start.56) | collective-permute-done | bytes 184352 | tf_op jit(solution)/shard_map/ppermute | solution.py:43
  (204 shorter events, 37.5 us)
Async XLA Ops:
  2.3 14.3 %collective-permute-start.10 = (bf16[24,1536]{1,0:T(8,128)(2,1)S(1)}, bf16[24,1536]{1,0:T(8,128)(2,1)S(1)}, u32[]{:S(2)}, u32[]{:S(2)}) collective-permute-start(bf16[24,1536]{1,0:T(8,128)(2,1)S(1)} %pad_maximum_fusion.10), channel_id=1, source_target_pairs={{0,1},{1,2},{2,3},{3,0},{4,5},{5,6},{6,7},{7,4},{8,9},{9,10},{10,1... | collective-permute-start | bytes 221192 | tf_op jit(solution)/shard_map/ppermute | solution.py:43
  5.3 14.1 %collective-permute-start.11 = (bf16[24,1536]{1,0:T(8,128)(2,1)S(1)}, bf16[24,1536]{1,0:T(8,128)(2,1)S(1)}, u32[]{:S(2)}, u32[]{:S(2)}) collective-permute-start(bf16[24,1536]{1,0:T(8,128)(2,1)S(1)} %pad_maximum_fusion.10), channel_id=1, source_target_pairs={{0,2},{1,3},{2,0},{3,1},{4,6},{5,7},{6,4},{7,5},{8,10},{9,11},{10,... | collective-permute-start | bytes 221192 | tf_op jit(solution)/shard_map/ppermute | solution.py:43
  7.9 12.1 %collective-permute-start.12 = (bf16[24,1536]{1,0:T(8,128)(2,1)S(1)}, bf16[24,1536]{1,0:T(8,128)(2,1)S(1)}, u32[]{:S(2)}, u32[]{:S(2)}) collective-permute-start(bf16[24,1536]{1,0:T(8,128)(2,1)S(1)} %pad_maximum_fusion.10), channel_id=1, source_target_pairs={{0,3},{1,0},{2,1},{3,2},{4,7},{5,4},{6,5},{7,6},{8,11},{9,8},{10,9... | collective-permute-start | bytes 221192 | tf_op jit(solution)/shard_map/ppermute | solution.py:43
  15.5 7.7 %collective-permute-start = (bf16[24,1664]{1,0:T(8,128)(2,1)S(1)}, bf16[24,1664]{1,0:T(8,128)(2,1)S(1)}, u32[]{:S(2)}, u32[]{:S(2)}) collective-permute-start(bf16[24,1664]{1,0:T(8,128)(2,1)S(1)} %concatenate.36), channel_id=1, source_target_pairs={{0,1},{1,2},{2,3},{3,0},{4,5},{5,6},{6,7},{7,4},{8,9},{9,10},{10,1... | collective-permute-start | bytes 239624 | tf_op jit(solution)/shard_map/ppermute | solution.py:43
  16.2 12.8 %collective-permute-start.1 = (bf16[24,1664]{1,0:T(8,128)(2,1)S(1)}, bf16[24,1664]{1,0:T(8,128)(2,1)S(1)}, u32[]{:S(2)}, u32[]{:S(2)}) collective-permute-start(bf16[24,1664]{1,0:T(8,128)(2,1)S(1)} %concatenate.36), channel_id=1, source_target_pairs={{0,2},{1,3},{2,0},{3,1},{4,6},{5,7},{6,4},{7,5},{8,10},{9,11},{10,... | collective-permute-start | bytes 239624 | tf_op jit(solution)/shard_map/ppermute | solution.py:43
  16.5 12.5 %collective-permute-start.2 = (bf16[24,1664]{1,0:T(8,128)(2,1)S(1)}, bf16[24,1664]{1,0:T(8,128)(2,1)S(1)}, u32[]{:S(2)}, u32[]{:S(2)}) collective-permute-start(bf16[24,1664]{1,0:T(8,128)(2,1)S(1)} %concatenate.36), channel_id=1, source_target_pairs={{0,3},{1,0},{2,1},{3,2},{4,7},{5,4},{6,5},{7,6},{8,11},{9,8},{10,9... | collective-permute-start | bytes 239624 | tf_op jit(solution)/shard_map/ppermute | solution.py:43
  19.4 12.2 %collective-permute-start.20 = (bf16[24,3072]{1,0:T(8,128)(2,1)}, bf16[24,3072]{1,0:T(8,128)(2,1)S(1)}, u32[]{:S(2)}, u32[]{:S(2)}) collective-permute-start(bf16[24,3072]{1,0:T(8,128)(2,1)} %param.20), channel_id=1, source_target_pairs={{0,1},{1,2},{2,3},{3,0},{4,5},{5,6},{6,7},{7,4},{8,9},{9,10},{10,1... | collective-permute-start | bytes 442376 | tf_op jit(solution)/shard_map/ppermute | solution.py:43
  20.0 21.7 %collective-permute-start.21 = (bf16[24,3072]{1,0:T(8,128)(2,1)}, bf16[24,3072]{1,0:T(8,128)(2,1)S(1)}, u32[]{:S(2)}, u32[]{:S(2)}) collective-permute-start(bf16[24,3072]{1,0:T(8,128)(2,1)} %param.20), channel_id=1, source_target_pairs={{0,2},{1,3},{2,0},{3,1},{4,6},{5,7},{6,4},{7,5},{8,10},{9,11},{10,... | collective-permute-start | bytes 442376 | tf_op jit(solution)/shard_map/ppermute | solution.py:43
  23.2 20.1 %collective-permute-start.22 = (bf16[24,3072]{1,0:T(8,128)(2,1)S(1)}, bf16[24,3072]{1,0:T(8,128)(2,1)S(1)}, u32[]{:S(2)}, u32[]{:S(2)}) collective-permute-start(bf16[24,3072]{1,0:T(8,128)(2,1)S(1)} %copy-done.9), channel_id=1, source_target_pairs={{0,3},{1,0},{2,1},{3,2},{4,7},{5,4},{6,5},{7,6},{8,11},{9,8},{10,9... | collective-permute-start | bytes 442376 | tf_op jit(solution)/shard_map/ppermute | solution.py:43
  29.0 15.7 %collective-permute-start.30 = (bf16[96,768]{1,0:T(8,128)(2,1)S(1)}, bf16[96,768]{1,0:T(8,128)(2,1)S(1)}, u32[]{:S(2)}, u32[]{:S(2)}) collective-permute-start(bf16[96,768]{1,0:T(8,128)(2,1)S(1)} %copy-done.10), channel_id=1, source_target_pairs={{0,1},{1,2},{2,3},{3,0},{4,5},{5,6},{6,7},{7,4},{8,9},{9,10},{10,1... | collective-permute-start | bytes 442376 | tf_op jit(solution)/shard_map/ppermute | solution.py:43
  29.0 19.0 %collective-permute-start.31 = (bf16[96,768]{1,0:T(8,128)(2,1)S(1)}, bf16[96,768]{1,0:T(8,128)(2,1)S(1)}, u32[]{:S(2)}, u32[]{:S(2)}) collective-permute-start(bf16[96,768]{1,0:T(8,128)(2,1)S(1)} %copy-done.10), channel_id=1, source_target_pairs={{0,2},{1,3},{2,0},{3,1},{4,6},{5,7},{6,4},{7,5},{8,10},{9,11},{10,... | collective-permute-start | bytes 442376 | tf_op jit(solution)/shard_map/ppermute | solution.py:43
  31.6 17.9 %collective-permute-start.32 = (bf16[96,768]{1,0:T(8,128)(2,1)S(1)}, bf16[96,768]{1,0:T(8,128)(2,1)S(1)}, u32[]{:S(2)}, u32[]{:S(2)}) collective-permute-start(bf16[96,768]{1,0:T(8,128)(2,1)S(1)} %copy-done.10), channel_id=1, source_target_pairs={{0,3},{1,0},{2,1},{3,2},{4,7},{5,4},{6,5},{7,6},{8,11},{9,8},{10,9... | collective-permute-start | bytes 442376 | tf_op jit(solution)/shard_map/ppermute | solution.py:43
  41.7 9.3 %collective-permute-start.16 = (bf16[96,1536]{1,0:T(8,128)(2,1)S(1)}, bf16[96,1536]{1,0:T(8,128)(2,1)S(1)}, u32[]{:S(2)}, u32[]{:S(2)}) collective-permute-start(bf16[96,1536]{1,0:T(8,128)(2,1)S(1)} %pad_maximum_fusion.5.rest_8_.rest_0_), channel_id=1, source_target_pairs={{0,16},{4,20},{8,24},{12,28},{16,0},{20,4},{24,8},{28,12},{1,17},{... | collective-permute-start | bytes 884744 | tf_op jit(solution)/shard_map/ppermute | solution.py:39
  43.2 7.8 %collective-permute-start.14 = (bf16[96,1536]{1,0:T(8,128)(2,1)S(1)}, bf16[96,1536]{1,0:T(8,128)(2,1)S(1)}, u32[]{:S(2)}, u32[]{:S(2)}) collective-permute-start(bf16[96,1536]{1,0:T(8,128)(2,1)S(1)} %pad_maximum_fusion.5.rest_8_.rest_0_), channel_id=1, source_target_pairs={{0,8},{4,12},{8,0},{12,4},{16,24},{20,28},{24,16},{28,20},{1,9},{5... | collective-permute-start | bytes 884744 | tf_op jit(solution)/shard_map/ppermute | solution.py:39
  44.7 7.2 %collective-permute-start.13 = (bf16[96,1536]{1,0:T(8,128)(2,1)S(1)}, bf16[96,1536]{1,0:T(8,128)(2,1)S(1)}, u32[]{:S(2)}, u32[]{:S(2)}) collective-permute-start(bf16[96,1536]{1,0:T(8,128)(2,1)S(1)} %pad_maximum_fusion.5.rest_8_.rest_0_), channel_id=1, source_target_pairs={{0,4},{4,0},{8,12},{12,8},{16,20},{20,16},{24,28},{28,24},{1,5},{5... | collective-permute-start | bytes 884744 | tf_op jit(solution)/shard_map/ppermute | solution.py:39
  48.0 10.5 %collective-permute-start.4 = (bf16[96,1664]{1,0:T(8,128)(2,1)S(1)}, bf16[96,1664]{1,0:T(8,128)(2,1)S(1)}, u32[]{:S(2)}, u32[]{:S(2)}) collective-permute-start(bf16[96,1664]{1,0:T(8,128)(2,1)S(1)} %pad_maximum_fusion.4.rest_0_), channel_id=1, source_target_pairs={{0,8},{4,12},{8,0},{12,4},{16,24},{20,28},{24,16},{28,20},{1,9},{5... | collective-permute-start | bytes 958472 | tf_op jit(solution)/shard_map/ppermute | solution.py:39
  49.5 10.5 %collective-permute-start.6 = (bf16[96,1664]{1,0:T(8,128)(2,1)S(1)}, bf16[96,1664]{1,0:T(8,128)(2,1)S(1)}, u32[]{:S(2)}, u32[]{:S(2)}) collective-permute-start(bf16[96,1664]{1,0:T(8,128)(2,1)S(1)} %pad_maximum_fusion.4.rest_0_), channel_id=1, source_target_pairs={{0,16},{4,20},{8,24},{12,28},{16,0},{20,4},{24,8},{28,12},{1,17},{... | collective-permute-start | bytes 958472 | tf_op jit(solution)/shard_map/ppermute | solution.py:39
  51.1 9.0 %collective-permute-start.3 = (bf16[96,1664]{1,0:T(8,128)(2,1)S(1)}, bf16[96,1664]{1,0:T(8,128)(2,1)S(1)}, u32[]{:S(2)}, u32[]{:S(2)}) collective-permute-start(bf16[96,1664]{1,0:T(8,128)(2,1)S(1)} %pad_maximum_fusion.4.rest_0_), channel_id=1, source_target_pairs={{0,4},{4,0},{8,12},{12,8},{16,20},{20,16},{24,28},{28,24},{1,5},{5... | collective-permute-start | bytes 958472 | tf_op jit(solution)/shard_map/ppermute | solution.py:39
  51.1 13.7 %collective-permute-start.18 = (bf16[96,1536]{1,0:T(8,128)(2,1)S(1)}, bf16[96,1536]{1,0:T(8,128)(2,1)S(1)}, u32[]{:S(2)}, u32[]{:S(2)}) collective-permute-start(bf16[96,1536]{1,0:T(8,128)(2,1)S(1)} %collective-permute-done.16.rest_12_.rest_4_), channel_id=1, source_target_pairs={{0,8},{4,12},{8,0},{12,4},{16,24},{20,28},{24,16},{28,20},{1,9},{5... | collective-permute-start | bytes 884744 | tf_op jit(solution)/shard_map/ppermute | solution.py:39
  51.9 13.0 %collective-permute-start.15 = (bf16[96,1536]{1,0:T(8,128)(2,1)S(1)}, bf16[96,1536]{1,0:T(8,128)(2,1)S(1)}, u32[]{:S(2)}, u32[]{:S(2)}) collective-permute-start(bf16[96,1536]{1,0:T(8,128)(2,1)S(1)} %collective-permute-done.14.rest_10_.rest_2_), channel_id=1, source_target_pairs={{0,4},{4,0},{8,12},{12,8},{16,20},{20,16},{24,28},{28,24},{1,5},{5... | collective-permute-start | bytes 884744 | tf_op jit(solution)/shard_map/ppermute | solution.py:39
  58.5 19.0 %collective-permute-start.24 = (bf16[96,3072]{1,0:T(8,128)(2,1)S(1)}, bf16[96,3072]{1,0:T(8,128)(2,1)S(1)}, u32[]{:S(2)}, u32[]{:S(2)}) collective-permute-start(bf16[96,3072]{1,0:T(8,128)(2,1)S(1)} %pad_maximum_fusion.1.rest_8_), channel_id=1, source_target_pairs={{0,8},{4,12},{8,0},{12,4},{16,24},{20,28},{24,16},{28,20},{1,9},{5... | collective-permute-start | bytes 1769480 | tf_op jit(solution)/shard_map/ppermute | solution.py:39
  60.0 5.6 %collective-permute-start.17 = (bf16[96,1536]{1,0:T(8,128)(2,1)S(1)}, bf16[96,1536]{1,0:T(8,128)(2,1)S(1)}, u32[]{:S(2)}, u32[]{:S(2)}) collective-permute-start(bf16[96,1536]{1,0:T(8,128)(2,1)S(1)} %collective-permute-done.16.rest_12_.rest_4_), channel_id=1, source_target_pairs={{0,4},{4,0},{8,12},{12,8},{16,20},{20,16},{24,28},{28,24},{1,5},{5... | collective-permute-start | bytes 884744 | tf_op jit(solution)/shard_map/ppermute | solution.py:39
  60.0 10.4 %collective-permute-start.8 = (bf16[96,1664]{1,0:T(8,128)(2,1)S(1)}, bf16[96,1664]{1,0:T(8,128)(2,1)S(1)}, u32[]{:S(2)}, u32[]{:S(2)}) collective-permute-start(bf16[96,1664]{1,0:T(8,128)(2,1)S(1)} %collective-permute-done.4.rest_2_), channel_id=1, source_target_pairs={{0,16},{4,20},{8,24},{12,28},{16,0},{20,4},{24,8},{28,12},{1,17},{... | collective-permute-start | bytes 958472 | tf_op jit(solution)/shard_map/ppermute | solution.py:39
  64.8 7.1 %collective-permute-start.5 = (bf16[96,1664]{1,0:T(8,128)(2,1)S(1)}, bf16[96,1664]{1,0:T(8,128)(2,1)S(1)}, u32[]{:S(2)}, u32[]{:S(2)}) collective-permute-start(bf16[96,1664]{1,0:T(8,128)(2,1)S(1)} %collective-permute-done.4.rest_2_), channel_id=1, source_target_pairs={{0,4},{4,0},{8,12},{12,8},{16,20},{20,16},{24,28},{28,24},{1,5},{5... | collective-permute-start | bytes 958472 | tf_op jit(solution)/shard_map/ppermute | solution.py:39
  64.9 7.6 %collective-permute-start.7 = (bf16[96,1664]{1,0:T(8,128)(2,1)S(1)}, bf16[96,1664]{1,0:T(8,128)(2,1)S(1)}, u32[]{:S(2)}, u32[]{:S(2)}) collective-permute-start(bf16[96,1664]{1,0:T(8,128)(2,1)S(1)} %collective-permute-done.6.rest_4_), channel_id=1, source_target_pairs={{0,4},{4,0},{8,12},{12,8},{16,20},{20,16},{24,28},{28,24},{1,5},{5... | collective-permute-start | bytes 958472 | tf_op jit(solution)/shard_map/ppermute | solution.py:39
  65.6 17.5 %collective-permute-start.36 = (bf16[384,768]{1,0:T(8,128)(2,1)S(1)}, bf16[384,768]{1,0:T(8,128)(2,1)S(1)}, u32[]{:S(2)}, u32[]{:S(2)}) collective-permute-start(bf16[384,768]{1,0:T(8,128)(2,1)S(1)} %pad_maximum_fusion.2.rest_16_), channel_id=1, source_target_pairs={{0,16},{4,20},{8,24},{12,28},{16,0},{20,4},{24,8},{28,12},{1,17},{... | collective-permute-start | bytes 1769480 | tf_op jit(solution)/shard_map/ppermute | solution.py:39
  70.4 24.9 %collective-permute-start.26 = (bf16[96,3072]{1,0:T(8,128)(2,1)S(1)}, bf16[96,3072]{1,0:T(8,128)(2,1)}, u32[]{:S(2)}, u32[]{:S(2)}) collective-permute-start(bf16[96,3072]{1,0:T(8,128)(2,1)S(1)} %pad_maximum_fusion.1.rest_8_), channel_id=1, source_target_pairs={{0,16},{4,20},{8,24},{12,28},{16,0},{20,4},{24,8},{28,12},{1,17},{... | collective-permute-start | bytes 1769480 | tf_op jit(solution)/shard_map/ppermute | solution.py:39
  72.0 23.4 %collective-permute-start.34 = (bf16[384,768]{1,0:T(8,128)(2,1)S(1)}, bf16[384,768]{1,0:T(8,128)(2,1)}, u32[]{:S(2)}, u32[]{:S(2)}) collective-permute-start(bf16[384,768]{1,0:T(8,128)(2,1)S(1)} %pad_maximum_fusion.2.rest_16_), channel_id=1, source_target_pairs={{0,8},{4,12},{8,0},{12,4},{16,24},{20,28},{24,16},{28,20},{1,9},{5... | collective-permute-start | bytes 1769480 | tf_op jit(solution)/shard_map/ppermute | solution.py:39
  72.5 24.9 %collective-permute-start.9 = (bf16[96,1664]{1,0:T(8,128)(2,1)S(1)}, bf16[96,1664]{1,0:T(8,128)(2,1)S(1)}, u32[]{:S(2)}, u32[]{:S(2)}) collective-permute-start(bf16[96,1664]{1,0:T(8,128)(2,1)S(1)} %collective-permute-done.8.rest_6_), channel_id=1, source_target_pairs={{0,4},{4,0},{8,12},{12,8},{16,20},{20,16},{24,28},{28,24},{1,5},{5... | collective-permute-start | bytes 958472 | tf_op jit(solution)/shard_map/ppermute | solution.py:39
  77.5 19.4 %collective-permute-start.19 = (bf16[96,1536]{1,0:T(8,128)(2,1)S(1)}, bf16[96,1536]{1,0:T(8,128)(2,1)S(1)}, u32[]{:S(2)}, u32[]{:S(2)}) collective-permute-start(bf16[96,1536]{1,0:T(8,128)(2,1)S(1)} %collective-permute-done.18.rest_14_.rest_6_), channel_id=1, source_target_pairs={{0,4},{4,0},{8,12},{12,8},{16,20},{20,16},{24,28},{28,24},{1,5},{5... | collective-permute-start | bytes 884744 | tf_op jit(solution)/shard_map/ppermute | solution.py:39
  83.1 25.3 %collective-permute-start.23 = (bf16[96,3072]{1,0:T(8,128)(2,1)S(1)}, bf16[96,3072]{1,0:T(8,128)(2,1)}, u32[]{:S(2)}, u32[]{:S(2)}) collective-permute-start(bf16[96,3072]{1,0:T(8,128)(2,1)S(1)} %pad_maximum_fusion.1.rest_8_), channel_id=1, source_target_pairs={{0,4},{4,0},{8,12},{12,8},{16,20},{20,16},{24,28},{28,24},{1,5},{5... | collective-permute-start | bytes 1769480 | tf_op jit(solution)/shard_map/ppermute | solution.py:39
  95.4 13.3 %collective-permute-start.33 = (bf16[384,768]{1,0:T(8,128)(2,1)S(1)}, bf16[384,768]{1,0:T(8,128)(2,1)}, u32[]{:S(2)}, u32[]{:S(2)}) collective-permute-start(bf16[384,768]{1,0:T(8,128)(2,1)S(1)} %pad_maximum_fusion.2.rest_16_), channel_id=1, source_target_pairs={{0,4},{4,0},{8,12},{12,8},{16,20},{20,16},{24,28},{28,24},{1,5},{5... | collective-permute-start | bytes 1769480 | tf_op jit(solution)/shard_map/ppermute | solution.py:39
  95.4 15.8 %collective-permute-start.28 = (bf16[96,3072]{1,0:T(8,128)(2,1)S(1)}, bf16[96,3072]{1,0:T(8,128)(2,1)}, u32[]{:S(2)}, u32[]{:S(2)}) collective-permute-start(bf16[96,3072]{1,0:T(8,128)(2,1)S(1)} %collective-permute-done.24.rest_10_), channel_id=1, source_target_pairs={{0,16},{4,20},{8,24},{12,28},{16,0},{20,4},{24,8},{28,12},{1,17},{... | collective-permute-start | bytes 1769480 | tf_op jit(solution)/shard_map/ppermute | solution.py:39
  96.9 15.6 %collective-permute-start.38 = (bf16[384,768]{1,0:T(8,128)(2,1)S(1)}, bf16[384,768]{1,0:T(8,128)(2,1)}, u32[]{:S(2)}, u32[]{:S(2)}) collective-permute-start(bf16[384,768]{1,0:T(8,128)(2,1)S(1)} %collective-permute-done.36.rest_20_), channel_id=1, source_target_pairs={{0,8},{4,12},{8,0},{12,4},{16,24},{20,28},{24,16},{28,20},{1,9},{5... | collective-permute-start | bytes 1769480 | tf_op jit(solution)/shard_map/ppermute | solution.py:39
  97.6 14.9 %collective-permute-start.25 = (bf16[96,3072]{1,0:T(8,128)(2,1)S(1)}, bf16[96,3072]{1,0:T(8,128)(2,1)}, u32[]{:S(2)}, u32[]{:S(2)}) collective-permute-start(bf16[96,3072]{1,0:T(8,128)(2,1)S(1)} %collective-permute-done.24.rest_10_), channel_id=1, source_target_pairs={{0,4},{4,0},{8,12},{12,8},{16,20},{20,16},{24,28},{28,24},{1,5},{5... | collective-permute-start | bytes 1769480 | tf_op jit(solution)/shard_map/ppermute | solution.py:39
  108.4 41.3 %collective-permute-start.37 = (bf16[384,768]{1,0:T(8,128)(2,1)S(1)}, bf16[384,768]{1,0:T(8,128)(2,1)}, u32[]{:S(2)}, u32[]{:S(2)}) collective-permute-start(bf16[384,768]{1,0:T(8,128)(2,1)S(1)} %collective-permute-done.36.rest_20_), channel_id=1, source_target_pairs={{0,4},{4,0},{8,12},{12,8},{16,20},{20,16},{24,28},{28,24},{1,5},{5... | collective-permute-start | bytes 1769480 | tf_op jit(solution)/shard_map/ppermute | solution.py:39
  108.7 41.0 %collective-permute-start.27 = (bf16[96,3072]{1,0:T(8,128)(2,1)}, bf16[96,3072]{1,0:T(8,128)(2,1)S(1)}, u32[]{:S(2)}, u32[]{:S(2)}) collective-permute-start(bf16[96,3072]{1,0:T(8,128)(2,1)} %collective-permute-done.26.rest_12_), channel_id=1, source_target_pairs={{0,4},{4,0},{8,12},{12,8},{16,20},{20,16},{24,28},{28,24},{1,5},{5... | collective-permute-start | bytes 1769480 | tf_op jit(solution)/shard_map/ppermute | solution.py:39
  111.2 38.5 %collective-permute-start.35 = (bf16[384,768]{1,0:T(8,128)(2,1)}, bf16[384,768]{1,0:T(8,128)(2,1)}, u32[]{:S(2)}, u32[]{:S(2)}) collective-permute-start(bf16[384,768]{1,0:T(8,128)(2,1)} %collective-permute-done.34.rest_18_), channel_id=1, source_target_pairs={{0,4},{4,0},{8,12},{12,8},{16,20},{20,16},{24,28},{28,24},{1,5},{5... | collective-permute-start | bytes 1769480 | tf_op jit(solution)/shard_map/ppermute | solution.py:39
  112.5 37.3 %collective-permute-start.29 = (bf16[96,3072]{1,0:T(8,128)(2,1)}, bf16[96,3072]{1,0:T(8,128)(2,1)}, u32[]{:S(2)}, u32[]{:S(2)}) collective-permute-start(bf16[96,3072]{1,0:T(8,128)(2,1)} %collective-permute-done.28.rest_14_), channel_id=1, source_target_pairs={{0,4},{4,0},{8,12},{12,8},{16,20},{20,16},{24,28},{28,24},{1,5},{5... | collective-permute-start | bytes 1769480 | tf_op jit(solution)/shard_map/ppermute | solution.py:39
  112.5 37.3 %collective-permute-start.39 = (bf16[384,768]{1,0:T(8,128)(2,1)}, bf16[384,768]{1,0:T(8,128)(2,1)S(1)}, u32[]{:S(2)}, u32[]{:S(2)}) collective-permute-start(bf16[384,768]{1,0:T(8,128)(2,1)} %collective-permute-done.38.rest_22_), channel_id=1, source_target_pairs={{0,4},{4,0},{8,12},{12,8},{16,20},{20,16},{24,28},{28,24},{1,5},{5... | collective-permute-start | bytes 1769480 | tf_op jit(solution)/shard_map/ppermute | solution.py:39
  260.6 2.4 collective-permute-start.46
  261.0 15.3 %collective-permute-start.40 = (bf16[4,96,1536]{2,1,0:T(8,128)(2,1)}, bf16[4,96,1536]{2,1,0:T(8,128)(2,1)S(1)}, u32[]{:S(2)}, u32[]{:S(2)}) collective-permute-start(bf16[4,96,1536]{2,1,0:T(8,128)(2,1)} %get-tuple-element.50), channel_id=1, source_target_pairs={{0,4},{4,0},{8,12},{12,8},{16,20},{20,16},{24,28},{28,24},{1,5},{5... | collective-permute-start | bytes 3538952 | tf_op jit(solution)/shard_map/ppermute | solution.py:39
  265.0 10.5 %collective-permute-start.47 = (bf16[2,96,896]{2,1,0:T(8,128)(2,1)}, bf16[2,96,896]{2,1,0:T(8,128)(2,1)S(1)}, u32[]{:S(2)}, u32[]{:S(2)}) collective-permute-start(bf16[2,96,896]{2,1,0:T(8,128)(2,1)} %stack.57), channel_id=1, source_target_pairs={{0,16},{4,20},{8,24},{12,28},{16,0},{20,4},{24,8},{28,12},{1,17},{... | collective-permute-start | bytes 1032200 | tf_op jit(solution)/shard_map/ppermute | solution.py:39
  265.6 34.1 %collective-permute-start.58 = (bf16[4,96,3072]{2,1,0:T(8,128)(2,1)}, bf16[4,96,3072]{2,1,0:T(8,128)(2,1)}, u32[]{:S(2)}, u32[]{:S(2)}) collective-permute-start(bf16[4,96,3072]{2,1,0:T(8,128)(2,1)} %get-tuple-element.56), channel_id=1, source_target_pairs={{0,4},{4,0},{8,12},{12,8},{16,20},{20,16},{24,28},{28,24},{1,5},{5... | collective-permute-start | bytes 7077896 | tf_op jit(solution)/shard_map/ppermute | solution.py:39
  275.6 7.4 %collective-permute-start.48 = (bf16[1,96,896]{2,1,0:T(8,128)(2,1)S(1)}, bf16[1,96,896]{2,1,0:T(8,128)(2,1)S(1)}, u32[]{:S(2)}, u32[]{:S(2)}) collective-permute-start(bf16[1,96,896]{2,1,0:T(8,128)(2,1)S(1)} %slice.147), channel_id=1, source_target_pairs={{0,8},{4,12},{8,0},{12,4},{16,24},{20,28},{24,16},{28,20},{1,9},{5... | collective-permute-start | bytes 516104 | tf_op jit(solution)/shard_map/ppermute | solution.py:39
  277.5 19.9 %collective-permute-start.41 = (bf16[2,96,1536]{2,1,0:T(8,128)(2,1)}, bf16[2,96,1536]{2,1,0:T(8,128)(2,1)}, u32[]{:S(2)}, u32[]{:S(2)}) collective-permute-start(bf16[2,96,1536]{2,1,0:T(8,128)(2,1)} %pad_maximum_fusion.3), channel_id=1, source_target_pairs={{0,8},{4,12},{8,0},{12,4},{16,24},{20,28},{24,16},{28,20},{1,9},{5... | collective-permute-start | bytes 1769480 | tf_op jit(solution)/shard_map/ppermute | solution.py:39
  284.4 6.2 %collective-permute-start.49 = (bf16[24,896]{1,0:T(8,128)(2,1)S(1)}, bf16[24,896]{1,0:T(8,128)(2,1)S(1)}, u32[]{:S(2)}, u32[]{:S(2)}) collective-permute-start(bf16[24,896]{1,0:T(8,128)(2,1)S(1)} %get-tuple-element.100), channel_id=1, source_target_pairs={{0,1},{1,2},{2,3},{3,0},{4,5},{5,6},{6,7},{7,4},{8,9},{9,10},{10,1... | collective-permute-start | bytes 129032 | tf_op jit(solution)/shard_map/ppermute | solution.py:43
  288.0 5.3 %collective-permute-start.50 = (bf16[24,896]{1,0:T(8,128)(2,1)}, bf16[24,896]{1,0:T(8,128)(2,1)}, u32[]{:S(2)}, u32[]{:S(2)}) collective-permute-start(bf16[24,896]{1,0:T(8,128)(2,1)} %get-tuple-element.102), channel_id=1, source_target_pairs={{0,2},{1,3},{2,0},{3,1},{4,6},{5,7},{6,4},{7,5},{8,10},{9,11},{10,... | collective-permute-start | bytes 129032 | tf_op jit(solution)/shard_map/ppermute | solution.py:43
  288.5 4.8 %collective-permute-start.51 = (bf16[24,896]{1,0:T(8,128)(2,1)}, bf16[24,896]{1,0:T(8,128)(2,1)}, u32[]{:S(2)}, u32[]{:S(2)}) collective-permute-start(bf16[24,896]{1,0:T(8,128)(2,1)} %get-tuple-element.101), channel_id=1, source_target_pairs={{0,3},{1,0},{2,1},{3,2},{4,7},{5,4},{6,5},{7,6},{8,11},{9,8},{10,9... | collective-permute-start | bytes 129032 | tf_op jit(solution)/shard_map/ppermute | solution.py:43
  291.2 19.4 %collective-permute-start.52 = (bf16[4,480,768]{2,1,0:T(8,128)(2,1)}, bf16[4,480,768]{2,1,0:T(8,128)(2,1)S(1)}, u32[]{:S(2)}, u32[]{:S(2)}) collective-permute-start(bf16[4,480,768]{2,1,0:T(8,128)(2,1)} %get-tuple-element.54), channel_id=1, source_target_pairs={{0,4},{4,0},{8,12},{12,8},{16,20},{20,16},{24,28},{28,24},{1,5},{5... | collective-permute-start | bytes 8847368 | tf_op jit(solution)/shard_map/ppermute | solution.py:39
  298.6 7.4 %collective-permute-start.42 = (bf16[1,96,1536]{2,1,0:T(8,128)(2,1)S(1)}, bf16[1,96,1536]{2,1,0:T(8,128)(2,1)S(1)}, u32[]{:S(2)}, u32[]{:S(2)}) collective-permute-start(bf16[1,96,1536]{2,1,0:T(8,128)(2,1)S(1)} %slice.145), channel_id=1, source_target_pairs={{0,16},{4,20},{8,24},{12,28},{16,0},{20,4},{24,8},{28,12},{1,17},{... | collective-permute-start | bytes 884744 | tf_op jit(solution)/shard_map/ppermute | solution.py:39
  302.6 25.9 %collective-permute-start.59 = (bf16[2,96,3072]{2,1,0:T(8,128)(2,1)S(1)}, bf16[2,96,3072]{2,1,0:T(8,128)(2,1)S(1)}, u32[]{:S(2)}, u32[]{:S(2)}) collective-permute-start(bf16[2,96,3072]{2,1,0:T(8,128)(2,1)S(1)} %pad_maximum_fusion), channel_id=1, source_target_pairs={{0,8},{4,12},{8,0},{12,4},{16,24},{20,28},{24,16},{28,20},{1,9},{5... | collective-permute-start | bytes 3538952 | tf_op jit(solution)/shard_map/ppermute | solution.py:39
  306.1 6.2 %collective-permute-start.43 = (bf16[24,1536]{1,0:T(8,128)(2,1)S(1)}, bf16[24,1536]{1,0:T(8,128)(2,1)S(1)}, u32[]{:S(2)}, u32[]{:S(2)}) collective-permute-start(bf16[24,1536]{1,0:T(8,128)(2,1)S(1)} %get-tuple-element.94), channel_id=1, source_target_pairs={{0,1},{1,2},{2,3},{3,0},{4,5},{5,6},{6,7},{7,4},{8,9},{9,10},{10,1... | collective-permute-start | bytes 221192 | tf_op jit(solution)/shard_map/ppermute | solution.py:43
  307.6 6.4 %collective-permute-start.44 = (bf16[24,1536]{1,0:T(8,128)(2,1)S(1)}, bf16[24,1536]{1,0:T(8,128)(2,1)S(1)}, u32[]{:S(2)}, u32[]{:S(2)}) collective-permute-start(bf16[24,1536]{1,0:T(8,128)(2,1)S(1)} %get-tuple-element.96), channel_id=1, source_target_pairs={{0,2},{1,3},{2,0},{3,1},{4,6},{5,7},{6,4},{7,5},{8,10},{9,11},{10,... | collective-permute-start | bytes 221192 | tf_op jit(solution)/shard_map/ppermute | solution.py:43
  309.3 5.2 %collective-permute-start.45 = (bf16[24,1536]{1,0:T(8,128)(2,1)S(1)}, bf16[24,1536]{1,0:T(8,128)(2,1)S(1)}, u32[]{:S(2)}, u32[]{:S(2)}) collective-permute-start(bf16[24,1536]{1,0:T(8,128)(2,1)S(1)} %get-tuple-element.95), channel_id=1, source_target_pairs={{0,3},{1,0},{2,1},{3,2},{4,7},{5,4},{6,5},{7,6},{8,11},{9,8},{10,9... | collective-permute-start | bytes 221192 | tf_op jit(solution)/shard_map/ppermute | solution.py:43
  311.6 35.3 %collective-permute-start.53 = (bf16[2,480,768]{2,1,0:T(8,128)(2,1)S(1)}, bf16[2,480,768]{2,1,0:T(8,128)(2,1)S(1)}, u32[]{:S(2)}, u32[]{:S(2)}) collective-permute-start(bf16[2,480,768]{2,1,0:T(8,128)(2,1)S(1)} %stack.59), channel_id=1, source_target_pairs={{0,16},{4,20},{8,24},{12,28},{16,0},{20,4},{24,8},{28,12},{1,17},{... | collective-permute-start | bytes 4423688 | tf_op jit(solution)/shard_map/ppermute | solution.py:39
  328.9 26.5 %collective-permute-start.60 = (bf16[1,96,3072]{2,1,0:T(8,128)(2,1)S(1)}, bf16[1,96,3072]{2,1,0:T(8,128)(2,1)S(1)}, u32[]{:S(2)}, u32[]{:S(2)}) collective-permute-start(bf16[1,96,3072]{2,1,0:T(8,128)(2,1)S(1)} %slice.158), channel_id=1, source_target_pairs={{0,16},{4,20},{8,24},{12,28},{16,0},{20,4},{24,8},{28,12},{1,17},{... | collective-permute-start | bytes 1769480 | tf_op jit(solution)/shard_map/ppermute | solution.py:39
  347.3 12.6 %collective-permute-start.54 = (bf16[1,480,768]{2,1,0:T(8,128)(2,1)S(1)}, bf16[1,480,768]{2,1,0:T(8,128)(2,1)S(1)}, u32[]{:S(2)}, u32[]{:S(2)}) collective-permute-start(bf16[1,480,768]{2,1,0:T(8,128)(2,1)S(1)} %slice.150), channel_id=1, source_target_pairs={{0,8},{4,12},{8,0},{12,4},{16,24},{20,28},{24,16},{28,20},{1,9},{5... | collective-permute-start | bytes 2211848 | tf_op jit(solution)/shard_map/ppermute | solution.py:39
  355.7 8.8 %collective-permute-start.61 = (bf16[24,3072]{1,0:T(8,128)(2,1)S(1)}, bf16[24,3072]{1,0:T(8,128)(2,1)S(1)}, u32[]{:S(2)}, u32[]{:S(2)}) collective-permute-start(bf16[24,3072]{1,0:T(8,128)(2,1)S(1)} %get-tuple-element.79), channel_id=1, source_target_pairs={{0,1},{1,2},{2,3},{3,0},{4,5},{5,6},{6,7},{7,4},{8,9},{9,10},{10,1... | collective-permute-start | bytes 442376 | tf_op jit(solution)/shard_map/ppermute | solution.py:43
  355.8 14.9 %collective-permute-start.62 = (bf16[24,3072]{1,0:T(8,128)(2,1)S(1)}, bf16[24,3072]{1,0:T(8,128)(2,1)S(1)}, u32[]{:S(2)}, u32[]{:S(2)}) collective-permute-start(bf16[24,3072]{1,0:T(8,128)(2,1)S(1)} %get-tuple-element.81), channel_id=1, source_target_pairs={{0,2},{1,3},{2,0},{3,1},{4,6},{5,7},{6,4},{7,5},{8,10},{9,11},{10,... | collective-permute-start | bytes 442376 | tf_op jit(solution)/shard_map/ppermute | solution.py:43
  358.0 12.7 %collective-permute-start.63 = (bf16[24,3072]{1,0:T(8,128)(2,1)S(1)}, bf16[24,3072]{1,0:T(8,128)(2,1)S(1)}, u32[]{:S(2)}, u32[]{:S(2)}) collective-permute-start(bf16[24,3072]{1,0:T(8,128)(2,1)S(1)} %get-tuple-element.80), channel_id=1, source_target_pairs={{0,3},{1,0},{2,1},{3,2},{4,7},{5,4},{6,5},{7,6},{8,11},{9,8},{10,9... | collective-permute-start | bytes 442376 | tf_op jit(solution)/shard_map/ppermute | solution.py:43
  360.2 13.6 %collective-permute-start.55 = (bf16[120,768]{1,0:T(8,128)(2,1)S(1)}, bf16[120,768]{1,0:T(8,128)(2,1)S(1)}, u32[]{:S(2)}, u32[]{:S(2)}) collective-permute-start(bf16[120,768]{1,0:T(8,128)(2,1)S(1)} %pad_maximum_fusion.7), channel_id=1, source_target_pairs={{0,1},{1,2},{2,3},{3,0},{4,5},{5,6},{6,7},{7,4},{8,9},{9,10},{10,1... | collective-permute-start | bytes 552968 | tf_op jit(solution)/shard_map/ppermute | solution.py:43
  360.5 21.1 %collective-permute-start.56 = (bf16[120,768]{1,0:T(8,128)(2,1)S(1)}, bf16[120,768]{1,0:T(8,128)(2,1)S(1)}, u32[]{:S(2)}, u32[]{:S(2)}) collective-permute-start(bf16[120,768]{1,0:T(8,128)(2,1)S(1)} %pad_maximum_fusion.8), channel_id=1, source_target_pairs={{0,2},{1,3},{2,0},{3,1},{4,6},{5,7},{6,4},{7,5},{8,10},{9,11},{10,... | collective-permute-start | bytes 552968 | tf_op jit(solution)/shard_map/ppermute | solution.py:43
  364.5 17.2 %collective-permute-start.57 = (bf16[120,768]{1,0:T(8,128)(2,1)S(1)}, bf16[120,768]{1,0:T(8,128)(2,1)S(1)}, u32[]{:S(2)}, u32[]{:S(2)}) collective-permute-start(bf16[120,768]{1,0:T(8,128)(2,1)S(1)} %pad_maximum_fusion.9), channel_id=1, source_target_pairs={{0,3},{1,0},{2,1},{3,2},{4,7},{5,4},{6,5},{7,6},{8,11},{9,8},{10,9... | collective-permute-start | bytes 552968 | tf_op jit(solution)/shard_map/ppermute | solution.py:43
  (32 other events, 626.8 us)
